TPU v7x, 128 devices: a whole 4x4x4 slice. The times are simulated.
128 devices in a mesh: dp: 32 (over z_lo, y, x), mp: 4 (over z_hi, core).
Axes of the slice: x: 4, y: 4, z: 4 (z_hi: 2, z_lo: 2; z = z_hi * 2 + z_lo), core: 2. Of those that a mesh axis runs over, the one named last changes fastest.
Arguments:
- pooled: bfloat16 [10240, 1792], P('dp'), may hold values from -6 to 6
- ln_gain: float32 [1792], replicated, may hold values from 0.5 to 1.5
- w_in: bfloat16 [15360, 1792], P(('dp', 'mp')), may hold values from -0.125 to 0.125
- w_out: bfloat16 [15360, 1792], P(('dp', 'mp')), may hold values from -0.046875 to 0.046875
- proj: bfloat16 [1792, 1024], replicated, may hold values from -0.125 to 0.125
- text: bfloat16 [10240, 1024], P(('dp', 'mp')), may hold values from -6 to 6
- logit_scale: float32 [1], replicated, may hold values from 5 to 15
- logit_bias: float32 [1], replicated, may hold values from -1 to 1
Outputs:
- d_pooled: float32 [10240, 1792], P(('dp', 'mp'))
- proj_grad: float32 [1792, 1024], P('dp', 'mp')
- text_grad: float32 [10240, 1024], P(('dp', 'mp'))
All inputs are finite; a program needn't handle non-finite values.
Results may differ from a plain program's by a relative error of at most 0.029.
Values may be sent and summed in bfloat16 or wider, within the bound.
A program may use at most 128 MiB of HBM per device.

v0:
```python
import jax
import jax.numpy as jnp
from jax import lax
from jax.sharding import PartitionSpec as P

STEPS = 4


def from_behind(block, axis, distance):
    devices = range(lax.axis_size(axis))
    route = [((i - distance) % len(devices), i) for i in devices]
    return lax.ppermute(block, axis, route)


def gelu_tanh(values):
    return jax.nn.gelu(values, approximate=True)


def per_device(pooled, ln_gain, w_in, w_out, proj, text, logit_scale, logit_bias):
    mp_index = lax.axis_index("mp")
    row_count = pooled.shape[0]
    share_rows = text.shape[0]
    column_count = proj.shape[1] // lax.axis_size("mp")
    hidden_f = pooled.astype(jnp.float32)
    center = hidden_f - jnp.mean(hidden_f, axis=-1, keepdims=True)
    inv_std = lax.rsqrt(jnp.mean(center * center, axis=-1, keepdims=True) + 1e-06)
    normed = center * inv_std
    x_in = (normed * ln_gain).astype(jnp.bfloat16)
    inputs_all, outputs_all = (
        lax.all_gather(w_in, "dp", axis=0, tiled=True),
        lax.all_gather(w_out, "dp", axis=0, tiled=True),
    )
    hidden_pre = jnp.einsum("bd,fd->bf", x_in, inputs_all, preferred_element_type=jnp.float32)
    hidden_act, gelu_back = jax.vjp(gelu_tanh, hidden_pre)
    act_bf = hidden_act.astype(jnp.bfloat16)
    mixed_part = jnp.dot(act_bf, outputs_all, preferred_element_type=jnp.float32)
    mixed = lax.psum(mixed_part, "mp")
    resid_bf = (hidden_f + mixed).astype(jnp.bfloat16)
    project = jnp.dot(resid_bf, proj, preferred_element_type=jnp.float32)
    inverse = lax.rsqrt(jnp.sum(project * project, axis=-1, keepdims=True) + 1e-06)
    unit_f = project * inverse
    embeds = unit_f.astype(jnp.bfloat16)
    text_f = text.astype(jnp.float32)
    text_inv = lax.rsqrt(jnp.sum(text_f * text_f, axis=-1, keepdims=True) + 1e-06)
    text_unit_f = text_f * text_inv
    text_unit = text_unit_f.astype(jnp.bfloat16)
    scaling = logit_scale[0]
    offset = logit_bias[0]
    positive = (
        jnp.arange(row_count, dtype=jnp.int32)[:, None]
        == mp_index * share_rows + jnp.arange(share_rows, dtype=jnp.int32)[None, :]
    )
    block = text_unit
    for step in range(STEPS):
        if step > 0:
            block = from_behind(block, "dp", 1)
            travel = from_behind(travel.astype(jnp.bfloat16), "dp", 1).astype(travel.dtype)
        logits = (
            scaling * jnp.einsum("me,ne->mn", embeds, block, preferred_element_type=jnp.float32)
            + offset
        )
        if step == 0:
            label = jnp.where(positive, 1.0, -1.0).astype(jnp.float32)
        else:
            label = -jnp.ones(logits.shape, jnp.float32)
        coef = (-label * jax.nn.sigmoid(-label * logits)).astype(jnp.bfloat16)
        image_term = scaling * jnp.dot(coef, block, preferred_element_type=jnp.float32)
        text_term = scaling * jnp.einsum(
            "mn,me->ne", coef, embeds, preferred_element_type=jnp.float32
        )
        image_term, text_term = (image_term, text_term)
        if step == 0:
            image_part = image_term
            travel = text_term
        else:
            image_part = image_part + image_term
            travel = travel + text_term
    unit_grad = from_behind(travel.astype(jnp.bfloat16), "dp", 1 - STEPS).astype(travel.dtype)
    text_grad = text_inv * (
        unit_grad - text_unit_f * jnp.sum(text_unit_f * unit_grad, axis=-1, keepdims=True)
    )
    embed_grad = lax.psum(image_part, "mp")
    inner = jnp.sum(unit_f * embed_grad, axis=-1, keepdims=True)
    proj_delta = (inverse * (embed_grad - unit_f * inner)).astype(jnp.bfloat16)
    resid_grad = jnp.einsum("me,de->md", proj_delta, proj, preferred_element_type=jnp.float32)
    delta_cols = lax.dynamic_slice_in_dim(proj_delta, mp_index * column_count, column_count, 1)
    proj_term = jnp.einsum("md,me->de", resid_bf, delta_cols, preferred_element_type=jnp.float32)
    proj_grad = lax.psum_scatter(
        proj_term.astype(jnp.bfloat16), "dp", scatter_dimension=0, tiled=True
    ).astype(jnp.float32)
    grad_bf = resid_grad.astype(jnp.bfloat16)
    act_grad = jnp.einsum("bd,fd->bf", grad_bf, outputs_all, preferred_element_type=jnp.float32)
    pre_grad = gelu_back(act_grad)[0].astype(jnp.bfloat16)
    input_part = jnp.dot(pre_grad, inputs_all, preferred_element_type=jnp.float32)
    input_grad = lax.psum_scatter(
        input_part.astype(jnp.bfloat16), "mp", scatter_dimension=0, tiled=True
    ).astype(jnp.float32)
    first_row = mp_index * share_rows
    normed_rows = lax.dynamic_slice_in_dim(normed, first_row, share_rows, 0)
    inv_rows = lax.dynamic_slice_in_dim(inv_std, first_row, share_rows, 0)
    resid_rows = lax.dynamic_slice_in_dim(resid_grad, first_row, share_rows, 0)
    scaled = input_grad * ln_gain
    shifted = scaled - jnp.mean(scaled, axis=-1, keepdims=True)
    shifted = shifted - normed_rows * jnp.mean(scaled * normed_rows, axis=-1, keepdims=True)
    d_pooled = resid_rows + inv_rows * shifted
    return (d_pooled, proj_grad, text_grad)


def solution(mesh):
    in_specs = (
        P("dp", None),
        P(),
        P(("dp", "mp"), None),
        P(("dp", "mp"), None),
        P(),
        P(("dp", "mp"), None),
        P(),
        P(),
    )
    out_specs = (P(("dp", "mp"), None), P("dp", "mp"), P(("dp", "mp"), None))
    return jax.shard_map(
        per_device, mesh=mesh, in_specs=in_specs, out_specs=out_specs, check_vma=False
    )
```

profile of v0, /device:TPU:1, one launch (start us, length us, event | category | flops | bytes accessed | tf_op | source)
XLA Modules:
  0.0 719.1 jit_solution(9060052048349454509)
XLA Ops:
  8.7 1.5 convert_reduce_fusion
  10.7 167.2 %all-gather.3.cloned.1.call-done = bf16[3840,1792]{1,0:T(8,128)(2,1)} async-done(((bf16[120,1792]{1,0:T(8,128)(2,1)}), bf16[3840,1792]{1,0:T(8,128)(2,1)}) %all-gather.3.cloned.1.call-update) | async-done | bytes 13762576 | tf_op jit(solution)/shard_map/all_gather | solution.py:30
  177.9 15.7 %fusion.24 = f32[320,3840]{1,0:T(8,128)} fusion(bf16[3840,1792]{1,0:T(8,128)(2,1)} %all-gather.3.cloned.1.call-done, f32[1792]{0:T(1024)S(1)} %copy-done.6, bf16[320,1792]{1,0:T(8,128)(2,1)S(1)} %copy-done, f32[320]{0:T(512)S(1)} %add_rsqrt_fusion.1, f32[320]{0:T(512)S(1)} %broadcast_multiply_fusion), kind=kOutput, calls=%fused_computation.43 | convolution fusion | flops 4406886400 | bytes 19834368 | tf_op jit(solution)/shard_map/bd,fd->bf/dot_general | solution.py:33
  193.6 165.0 %all-gather.5.cloned.1.call-done = bf16[3840,1792]{1,0:T(8,128)(2,1)} async-done(((bf16[120,1792]{1,0:T(8,128)(2,1)}), bf16[3840,1792]{1,0:T(8,128)(2,1)}) %all-gather.5.cloned.1.call-update) | async-done | bytes 13762576 | tf_op jit(solution)/shard_map/all_gather | solution.py:31
  358.6 13.2 %fusion.9 = f32[320,1792]{1,0:T(8,128)} fusion(bf16[3840,1792]{1,0:T(8,128)(2,1)} %all-gather.5.cloned.1.call-done, f32[320,3840]{1,0:T(8,128)} %fusion.24), kind=kOutput, calls=%fused_computation.17 | convolution fusion | flops 4415078400 | bytes 20971520 | tf_op jit(solution)/shard_map/dot_general | solution.py:36
  373.1 8.4 %collective-permute-done = bf16[80,1024]{1,0:T(8,128)(2,1)S(1)} collective-permute-done((bf16[80,1024]{1,0:T(8,128)(2,1)S(1)}, bf16[80,1024]{1,0:T(8,128)(2,1)S(1)}, u32[]{:S(2)}, u32[]{:S(2)}) %collective-permute-start) | collective-permute-done | bytes 163872 | tf_op jit(solution)/shard_map/ppermute | solution.py:12
  382.8 7.2 collective-permute-done.1
  390.0 60.2 %all-reduce.3.cloned.1.call-done = f32[320,1792]{1,0:T(8,128)} async-done(((f32[320,1792]{1,0:T(8,128)}), f32[320,1792]{1,0:T(8,128)}) %all-reduce.3.cloned.1.call-update) | async-done | bytes 2293776 | tf_op jit(solution)/shard_map/psum | solution.py:37
  450.1 4.2 multiply_reduce_fusion.1
  455.6 1.3 fusion.56
  457.3 1.3 convolution_add_fusion.1
  458.6 1.3 fusion.57
  459.8 2.3 fusion.22
  462.3 0.9 fusion.23
  463.2 1.2 collective-permute-start.3
  464.4 44.9 %all-reduce.5.cloned.1.call-done = f32[320,1024]{1,0:T(8,128)} async-done(((f32[320,1024]{1,0:T(8,128)}), f32[320,1024]{1,0:T(8,128)}) %all-reduce.5.cloned.1.call-update) | async-done | bytes 1310736 | tf_op jit(solution)/shard_map/psum | solution.py:82
  509.3 1.8 multiply_reduce_fusion
  512.2 2.8 fusion.81
  514.9 1.7 convolution_convert_fusion.1
  516.6 17.7 %convolution_convert_fusion = bf16[320,1792]{1,0:T(8,128)(2,1)} fusion(bf16[3840,1792]{1,0:T(8,128)(2,1)} %all-gather.3.cloned.1.call-done, f32[320,3840]{1,0:T(8,128)} %fusion.24, bf16[3840,1792]{1,0:T(8,128)(2,1)} %all-gather.5.cloned.1.call-done, f32[320,1792]{1,0:T(8,128)} %fusion.81), kind=kOutput, calls=%fused_computation.15 | convolution fusion | flops 8833761280 | bytes 35880960 | tf_op jit(solution)/shard_map/dot_general | solution.py:94
  534.3 1.2 add_convert_fusion.2
  535.5 1.3 collective-permute-start.4
  537.1 8.5 %collective-permute-done.4 = bf16[80,1024]{1,0:T(8,128)(2,1)S(1)} collective-permute-done((bf16[80,1024]{1,0:T(8,128)(2,1)S(1)}, bf16[80,1024]{1,0:T(8,128)(2,1)S(1)}, u32[]{:S(2)}, u32[]{:S(2)}) %collective-permute-start.4) | collective-permute-done | bytes 163872 | tf_op jit(solution)/shard_map/ppermute | solution.py:12
  546.0 9.0 %collective-permute-done.5 = bf16[80,1024]{1,0:T(8,128)(2,1)S(1)} collective-permute-done((bf16[80,1024]{1,0:T(8,128)(2,1)S(1)}, bf16[80,1024]{1,0:T(8,128)(2,1)S(1)}, u32[]{:S(2)}, u32[]{:S(2)}) %collective-permute-start.5) | collective-permute-done | bytes 163872 | tf_op jit(solution)/shard_map/ppermute | solution.py:12
  556.1 5.3 collective-permute-done.6
  561.4 1.2 fusion.62
  562.6 1.9 fusion.63
  564.5 88.7 %reduce-scatter.5.cloned.1.call-done = bf16[56,256]{1,0:T(8,128)(2,1)} async-done(((bf16[1792,256]{1,0:T(8,128)(2,1)}), bf16[56,256]{1,0:T(8,128)(2,1)}) %reduce-scatter.5.cloned.1.call-update) | async-done | bytes 28688 | tf_op jit(solution)/shard_map/reduce_scatter | solution.py:88
  653.2 1.4 convert_element_type.95
  654.6 54.3 %reduce-scatter.3.cloned.1.call-done = bf16[80,1792]{1,0:T(8,128)(2,1)} async-done(((bf16[320,1792]{1,0:T(8,128)(2,1)}), bf16[80,1792]{1,0:T(8,128)(2,1)}) %reduce-scatter.3.cloned.1.call-update) | async-done | bytes 286736 | tf_op jit(solution)/shard_map/reduce_scatter | solution.py:95
  708.9 1.1 fusion.58
  710.1 2.2 multiply_add_fusion
  (56 shorter events, 7.8 us)
Async XLA Ops:
  7.2 3.1 copy-start
  7.2 170.7 %copy-start.6 = (f32[1792]{0:T(1024)S(1)}, f32[1792]{0:T(1024)}, u32[]{:S(2)}) copy-start(f32[1792]{0:T(1024)} %param.9) | copy-start | bytes 21508
  7.2 170.7 %all-gather.3.cloned.1.call-start = ((), (), s32[]{:S(2)}) async-start(), calls=%async_computation.2 | async-start | bytes 14192640 | tf_op jit(solution)/shard_map/all_gather | solution.py:30
  7.9 350.7 %all-gather.5.cloned.1.call-start = ((), (), s32[]{:S(2)}) async-start(), calls=%async_computation.3 | async-start | bytes 14192640 | tf_op jit(solution)/shard_map/all_gather | solution.py:31
  8.7 441.5 %all-reduce.3.cloned.1.call-start = ((), (), s32[]{:S(2)}) async-start(), calls=%async_computation.4 | async-start | bytes 4587520 | tf_op jit(solution)/shard_map/psum | solution.py:37
  371.8 0.9 copy-start.2
  371.9 137.5 %all-reduce.5.cloned.1.call-start = ((), (), s32[]{:S(2)}) async-start(), calls=%async_computation.5 | async-start | bytes 2621440 | tf_op jit(solution)/shard_map/psum | solution.py:82
  373.0 8.5 %collective-permute-start = (bf16[80,1024]{1,0:T(8,128)(2,1)S(1)}, bf16[80,1024]{1,0:T(8,128)(2,1)S(1)}, u32[]{:S(2)}, u32[]{:S(2)}) collective-permute-start(bf16[80,1024]{1,0:T(8,128)(2,1)S(1)} %fusion.60), channel_id=1, source_target_pairs={{124,0},{0,4},{4,8},{8,12},{12,16},{16,20},{20,24},{24,28},{28,32}... | collective-permute-start | bytes 491528 | tf_op jit(solution)/shard_map/ppermute | solution.py:12
  381.5 72.8 %copy-start.4 = (bf16[80,1024]{1,0:T(8,128)(2,1)}, bf16[80,1024]{1,0:T(8,128)(2,1)S(1)}, u32[]{:S(2)}) copy-start(bf16[80,1024]{1,0:T(8,128)(2,1)S(1)} %collective-permute-done) | copy-start | bytes 491524
  381.5 8.5 %collective-permute-start.1 = (bf16[80,1024]{1,0:T(8,128)(2,1)S(1)}, bf16[80,1024]{1,0:T(8,128)(2,1)}, u32[]{:S(2)}, u32[]{:S(2)}) collective-permute-start(bf16[80,1024]{1,0:T(8,128)(2,1)S(1)} %collective-permute-done), channel_id=1, source_target_pairs={{124,0},{0,4},{4,8},{8,12},{12,16},{16,20},{20,24},{24,28},{28,32}... | collective-permute-start | bytes 491528 | tf_op jit(solution)/shard_map/ppermute | solution.py:12
  390.0 68.6 %collective-permute-start.2 = (bf16[80,1024]{1,0:T(8,128)(2,1)}, bf16[80,1024]{1,0:T(8,128)(2,1)}, u32[]{:S(2)}, u32[]{:S(2)}) collective-permute-start(bf16[80,1024]{1,0:T(8,128)(2,1)} %collective-permute-done.1), channel_id=1, source_target_pairs={{124,0},{0,4},{4,8},{8,12},{12,16},{16,20},{20,24},{24,28},{28,32}... | collective-permute-start | bytes 491528 | tf_op jit(solution)/shard_map/ppermute | solution.py:12
  454.3 0.9 copy-start.5
  462.2 191.0 %reduce-scatter.5.cloned.1.call-start = ((), (), s32[]{:S(2)}) async-start(), calls=%async_computation.7 | async-start | bytes 946176 | tf_op jit(solution)/shard_map/reduce_scatter | solution.py:88
  463.2 71.1 %collective-permute-start.3 = (bf16[80,1024]{1,0:T(8,128)(2,1)}, bf16[80,1024]{1,0:T(8,128)(2,1)}, u32[]{:S(2)}, u32[]{:S(2)}) collective-permute-start(bf16[80,1024]{1,0:T(8,128)(2,1)} %fusion.23), channel_id=1, source_target_pairs={{124,0},{0,4},{4,8},{8,12},{12,16},{16,20},{20,24},{24,28},{28,32}... | collective-permute-start | bytes 491528 | tf_op jit(solution)/shard_map/ppermute | solution.py:12
  509.3 1.8 copy-start.1
  509.3 2.8 copy-start.7
  512.2 2.8 copy-start.3
  516.6 192.3 %reduce-scatter.3.cloned.1.call-start = ((), (), s32[]{:S(2)}) async-start(), calls=%async_computation.6 | async-start | bytes 1433600 | tf_op jit(solution)/shard_map/reduce_scatter | solution.py:95
  535.5 10.1 %collective-permute-start.4 = (bf16[80,1024]{1,0:T(8,128)(2,1)S(1)}, bf16[80,1024]{1,0:T(8,128)(2,1)S(1)}, u32[]{:S(2)}, u32[]{:S(2)}) collective-permute-start(bf16[80,1024]{1,0:T(8,128)(2,1)S(1)} %add_convert_fusion.2), channel_id=1, source_target_pairs={{124,0},{0,4},{4,8},{8,12},{12,16},{16,20},{20,24},{24,28},{28,32}... | collective-permute-start | bytes 491528 | tf_op jit(solution)/shard_map/ppermute | solution.py:12
  545.7 9.3 %collective-permute-start.5 = (bf16[80,1024]{1,0:T(8,128)(2,1)S(1)}, bf16[80,1024]{1,0:T(8,128)(2,1)S(1)}, u32[]{:S(2)}, u32[]{:S(2)}) collective-permute-start(bf16[80,1024]{1,0:T(8,128)(2,1)S(1)} %add_convert_fusion.1), channel_id=1, source_target_pairs={{124,0},{0,4},{4,8},{8,12},{12,16},{16,20},{20,24},{24,28},{28,32}... | collective-permute-start | bytes 491528 | tf_op jit(solution)/shard_map/ppermute | solution.py:12
  555.7 5.7 collective-permute-start.6
Sparse Core Ops, SparseCore 0:
  9.7 168.1 all-gather.2
  179.5 179.0 all-gather.4
  372.0 78.0 all-reduce.2
  462.3 46.9 all-reduce.4
  516.7 136.4 reduce-scatter.4
  655.7 53.1 reduce-scatter.2
where the time goes:
time: 720 us; the launch traced here: 719 us
  waiting for transfers between devices  620 us (86%)
  matrix products  65.5 us (9%)
  between operations  15.6 us (2%)
  other arithmetic  13.3 us (2%)
    all_gather x1, waiting for transfers between devices, per_device(): lax.all_gather(w_in, 'dp', axis=0, tiled=True)  167 us
    all_gather x1, waiting for transfers between devices, per_device(): lax.all_gather(w_out, 'dp', axis=0, tiled=True)  165 us
    reduce_scatter x1, waiting for transfers between devices, per_device(): lax.psum_scatter(proj_term.astype(jnp.bfloat16), 'dp', scatter_dimension=...  88.7 us
    psum x1, waiting for transfers between devices, per_device(): mixed = lax.psum(mixed_part, 'mp')  60.2 us
    reduce_scatter x1, waiting for transfers between devices, per_device(): lax.psum_scatter(input_part.astype(jnp.bfloat16), 'mp', scatter_dimension...  54.3 us
    psum x1, waiting for transfers between devices, per_device(): embed_grad = lax.psum(image_part, 'mp')  44.9 us
    ppermute x7, waiting for transfers between devices, from_behind(): return lax.ppermute(block, axis, route)  38.3 us
    dot_general x1, matrix products, per_device(): jnp.dot(pre_grad, inputs_all, preferred_element_type=jnp.float32)  17.7 us
  transfers between devices with their start and end apart: 13, of which 11 were waited for; matrix products, arithmetic and copies ran while one was open for 8% of the time, Pallas kernels for 0%

commit v1 on v0

v1 whole, which is shorter than its diff:
```python
import functools

import jax
import jax.numpy as jnp
from jax import lax
from jax.experimental import pallas as pl
from jax.experimental.pallas import tpu as pltpu
from jax.sharding import PartitionSpec as P

D = 1792
H = D // 2
E = 1024
U = 120
R = 80
F32 = jnp.float32
BF16 = jnp.bfloat16
MESH = pl.DeviceIdType.MESH
PAIRS = (
    ((0, 0), (3, 0)),
    ((1, 0), (0, 3)),
    ((0, 1), (3, 3)),
    ((3, 1), (1, 3)),
    ((1, 1), (2, 0)),
    ((0, 2), (2, 3)),
    ((2, 1), (3, 2)),
    ((1, 2), (2, 2)),
)
N_SEMS = 128


def mm(a, b):
    return lax.dot_general(a, b, (((1,), (0,)), ((), ())), preferred_element_type=F32)


def mm_nt(a, b):
    return lax.dot_general(a, b, (((1,), (1,)), ((), ())), preferred_element_type=F32)


def mm_tn(a, b):
    return lax.dot_general(a, b, (((0,), (0,)), ((), ())), preferred_element_type=F32)


def gelu_and_slope(v):
    c = 0.7978845608028654
    v2 = v * v
    t = jnp.tanh(c * v * (1.0 + 0.044715 * v2))
    half = 0.5 * (1.0 + t)
    act = v * half
    slope = half + (0.5 * v) * (1.0 - t * t) * (c * (1.0 + 3.0 * 0.044715 * v2))
    return act, slope


def kernel(
    pooled, gain, w_in, w_out, proj_hbm, text, scale, bias,
    d_pooled, proj_grad, text_grad,
    slot_in, slot_out, dense_in, dense_out, x, acc, slope, grad_bf, resid_grad,
    tall, eall, proj, stage, core_in, hop, fin, direct, pd, resid_bf, rs, rs_hop,
    pg, pg_in, pg2, pg2_in, send_sems, recv_sems, local_sems,
):
    dp = lax.axis_index("dp")
    mp = lax.axis_index("mp")
    z_lo = dp // 16
    yi = (dp // 4) % 4
    xi = dp % 4
    z_hi = mp // 2
    c = mp % 2
    z = z_hi * 2 + z_lo

    def place(dx=0, dy=0, dz=0, other=False):
        nz = (z + dz) % 4
        ndp = (nz % 2) * 16 + ((yi + dy) % 4) * 4 + (xi + dx) % 4
        nmp = (nz // 2) * 2 + (1 - c if other else c)
        return {"dp": ndp, "mp": nmp}

    def shifted(k):
        return {"dp": (dp + k + 32) % 32, "mp": mp}

    x_fwd, x_bwd, x_far = place(dx=1), place(dx=3), place(dx=2)
    y_fwd, y_bwd, y_far = place(dy=1), place(dy=3), place(dy=2)
    z_fwd, z_bwd, z_far = place(dz=1), place(dz=3), place(dz=2)
    core = place(other=True)

    count = [0]
    started = []

    def send(src, dst, where):
        n = count[0]
        count[0] += 1
        copy = pltpu.make_async_remote_copy(
            src_ref=src, dst_ref=dst, send_sem=send_sems.at[n], recv_sem=recv_sems.at[n],
            device_id=where, device_id_type=MESH,
        )
        copy.start()
        started.append(copy)
        return copy

    def slot(dx, dy):
        return dy * 4 + dx

    locals_ = [
        pltpu.make_async_copy(w_in, slot_in.at[0], local_sems.at[0]),
        pltpu.make_async_copy(w_out, slot_out.at[0], local_sems.at[1]),
        pltpu.make_async_copy(proj_hbm, proj, local_sems.at[2]),
    ]
    for copy in locals_:
        copy.start()

    peers = [x_fwd, x_bwd, x_far, y_fwd, y_bwd, y_far, z_fwd, z_bwd, z_far, core]
    peers += [shifted(k) for k in (-3, -2, -1, 1, 2, 3)]
    barrier = pltpu.get_barrier_semaphore()
    for peer in peers:
        pl.semaphore_signal(barrier, inc=1, device_id=peer, device_id_type=MESH)
    pl.semaphore_wait(barrier, len(peers))

    arrive = {}

    def give(which, ref, src, dst_slot, where, half=None):
        if half is None:
            target = ref.at[dst_slot]
            source = src
        else:
            columns = pl.ds(half * H, H)
            target = ref.at[dst_slot, :, columns]
            source = src.at[:, columns]
        arrive[which, dst_slot, half] = send(source, target, where)

    A, B = ("in", slot_in), ("out", slot_out)
    give(*A, w_in, slot(3, 0), x_fwd)
    give(*A, w_in, slot(1, 0), x_bwd)
    give(*B, w_out, slot(0, 3), y_fwd)
    give(*B, w_out, slot(0, 1), y_bwd)
    give(*B, w_out, slot(3, 0), x_fwd)
    give(*B, w_out, slot(1, 0), x_bwd)
    give(*A, w_in, slot(0, 3), y_fwd)
    give(*A, w_in, slot(0, 1), y_bwd)

    def text_parts():
        t = text[...].astype(F32)
        inv = lax.rsqrt(jnp.sum(t * t, axis=-1, keepdims=True) + 1e-06)
        return t * inv, inv

    tall[0, 0] = text_parts()[0].astype(BF16)
    text_first = [send(tall.at[0, 0], tall.at[0, k], shifted(k)) for k in (1, 2, 3)]

    def norm_rows(start):
        h = pooled[pl.ds(pl.multiple_of(start, 16), R), :].astype(F32)
        center = h - jnp.mean(h, axis=-1, keepdims=True)
        inv_std = lax.rsqrt(jnp.mean(center * center, axis=-1, keepdims=True) + 1e-06)
        return h, center * inv_std, inv_std

    own_row = z_hi * 160 + c * R
    other_row = z_hi * 160 + (1 - c) * R
    far_own = (1 - z_hi) * 160 + c * R
    far_other = (1 - z_hi) * 160 + (1 - c) * R

    def fill_x(dz, j, start):
        x[dz, j * R:(j + 1) * R, :] = (norm_rows(start)[1] * gain[...]).astype(BF16)

    fill_x(0, 0, own_row)
    fill_x(0, 1, other_row)
    x_up = send(x.at[0], x.at[3], z_fwd)
    x_down = send(x.at[0], x.at[1], z_bwd)
    fill_x(2, 0, far_own)
    fill_x(2, 1, far_other)

    def got(which, where, half=None):
        arrive[which, slot(*where), half].wait_recv()

    def spread(which, ref, where, axis, half_also=True):
        dx, dy = where
        src = ref.at[slot(dx, dy)]
        if axis == "y":
            give(which, ref, src, slot(dx, 3), y_fwd)
            give(which, ref, src, slot(dx, 1), y_bwd)
        else:
            give(which, ref, src, slot(3, dy), x_fwd)
            give(which, ref, src, slot(1, dy), x_bwd)

    def pass_on(which, ref, where, axis):
        dx, dy = where
        src = ref.at[slot(dx, dy)]
        if axis == "x":
            if dx == 3:
                give(which, ref, src, slot(2, dy), x_fwd, 0)
            else:
                give(which, ref, src, slot(2, dy), x_bwd, 1)
        else:
            if dy == 3:
                give(which, ref, src, slot(dx, 2), y_fwd, 0)
            else:
                give(which, ref, src, slot(dx, 2), y_bwd, 1)

    def both_halves(which, where):
        got(which, where, 0)
        got(which, where, 1)

    def pack_pair(p):
        s0, s1 = slot(*PAIRS[p][0]), slot(*PAIRS[p][1])
        for ref, dense in ((slot_in, dense_in), (slot_out, dense_out)):
            both = jnp.concatenate([ref[s0].astype(F32), ref[s1].astype(F32)], axis=0)
            dense[p] = both.astype(BF16)

    def forward_pair(p):
        pack_pair(p)

        @pl.loop(0, 2)
        def _(i):
            rows = pl.ds(2 * i, 2)
            pre = mm_nt(x[rows].reshape(4 * R, D), dense_in[p])
            act, der = gelu_and_slope(pre)
            slope[p, rows] = der.astype(slope.dtype).reshape(2, 2 * R, 2 * U)
            act = act.astype(BF16)
            for n in range(0, D, 256):
                part = mm(act, dense_out[p, :, n:n + 256]).reshape(2, 2 * R, 256)
                if p == 0:
                    acc[rows, :, n:n + 256] = part
                else:
                    acc[rows, :, n:n + 256] += part

    for dx in (3, 1):
        got("in", (dx, 0))
        pass_on(*A, (dx, 0), "x")
    for dy in (3, 1):
        got("out", (0, dy))
        pass_on(*B, (0, dy), "y")
    for dx in (3, 1):
        spread(*A, (dx, 0), "y")
    for dy in (3, 1):
        spread(*B, (0, dy), "x")
    for copy in locals_:
        copy.wait()
    for dy in (3, 1):
        got("in", (0, dy))
        pass_on(*A, (0, dy), "y")
    for dx in (3, 1):
        got("out", (dx, 0))
        pass_on(*B, (dx, 0), "x")
    x_up.wait_recv()
    x_down.wait_recv()
    for copy in text_first:
        copy.wait_recv()
    text_far = send(tall.at[0], tall.at[1], z_far)
    text_core = send(tall.at[0], tall.at[2], core)
    forward_pair(0)
    both_halves("in", (2, 0))
    spread(*A, (2, 0), "y")
    both_halves("out", (0, 2))
    spread(*B, (0, 2), "x")
    forward_pair(1)
    for dx in (3, 1):
        for dy in (3, 1):
            got("in", (dx, dy))
            pass_on(*A, (dx, dy), "y")
    for dy in (3, 1):
        for dx in (3, 1):
            got("out", (dx, dy))
            pass_on(*B, (dx, dy), "x")
    forward_pair(2)
    text_far.wait_recv()
    text_far_core = send(tall.at[1], tall.at[3], core)
    forward_pair(3)
    both_halves("in", (0, 2))
    both_halves("out", (2, 0))
    for dy in (3, 1):
        got("in", (2, dy))
        pass_on(*A, (2, dy), "y")
    for dx in (3, 1):
        got("out", (dx, 2))
        pass_on(*B, (dx, 2), "x")
    forward_pair(4)
    both_halves("out", (2, 3))
    forward_pair(5)
    both_halves("out", (2, 1))
    both_halves("in", (3, 2))
    forward_pair(6)
    both_halves("in", (1, 2))
    both_halves("in", (2, 2))
    both_halves("out", (2, 2))
    forward_pair(7)

    lo, hi = slice(0, H), slice(H, D)

    def reduce_rows(turn):
        from_core = {}
        for dz in (2, 1, 3, 0):
            stage[turn, dz] = acc[dz, R:2 * R, :].astype(BF16)
            from_core[dz] = send(stage.at[turn, dz], core_in.at[turn, dz], core)
        from_core[2].wait_recv()
        direct[turn, 0] = (acc[2, :R, :] + core_in[turn, 2].astype(F32)).astype(BF16)
        hop_up = send(direct.at[turn, 0, :, lo], hop.at[turn, 0], z_fwd)
        hop_down = send(direct.at[turn, 0, :, hi], hop.at[turn, 1], z_bwd)
        from_core[1].wait_recv()
        up = acc[1, :R, :] + core_in[turn, 1].astype(F32)
        acc[1, :R, :] = up
        direct[turn, 1, :, hi] = up[:, hi].astype(BF16)
        up_hi = send(direct.at[turn, 1, :, hi], fin.at[turn, 0, :, hi], z_fwd)
        from_core[3].wait_recv()
        down = acc[3, :R, :] + core_in[turn, 3].astype(F32)
        acc[3, :R, :] = down
        direct[turn, 2, :, lo] = down[:, lo].astype(BF16)
        down_lo = send(direct.at[turn, 2, :, lo], fin.at[turn, 1, :, lo], z_bwd)
        from_core[0].wait_recv()
        acc[0, :R, :] += core_in[turn, 0].astype(F32)
        hop_up.wait_recv()
        direct[turn, 1, :, lo] = (acc[1, :R, lo] + hop[turn, 0].astype(F32)).astype(BF16)
        up_lo = send(direct.at[turn, 1, :, lo], fin.at[turn, 0, :, lo], z_fwd)
        hop_down.wait_recv()
        direct[turn, 2, :, hi] = (acc[3, :R, hi] + hop[turn, 1].astype(F32)).astype(BF16)
        down_hi = send(direct.at[turn, 2, :, hi], fin.at[turn, 1, :, hi], z_bwd)
        return up_hi, down_lo, up_lo, down_hi

    def reduced(turn, pending):
        for copy in pending:
            copy.wait_recv()
        return acc[0, :R, :] + fin[turn, 0].astype(F32) + fin[turn, 1].astype(F32)

    pending = reduce_rows(0)
    mixed = reduced(0, pending)
    pooled_rows = pooled[pl.ds(pl.multiple_of(own_row, 16), R), :].astype(F32)
    resid_bf[...] = (pooled_rows + mixed).astype(BF16)

    own_cols = pl.ds(pl.multiple_of(z_lo * H, 128), H)
    other_cols = pl.ds(pl.multiple_of((1 - z_lo) * H, 128), H)
    rs[0, 0] = resid_bf[:, own_cols]
    rs_up = send(resid_bf.at[:, other_cols], rs.at[0, 3], z_fwd)
    rs_down = send(resid_bf.at[:, other_cols], rs.at[0, 1], z_bwd)
    rs_hop_up = send(resid_bf.at[0:48, own_cols], rs_hop.at[0:48], z_fwd)
    rs_hop_down = send(resid_bf.at[48:80, own_cols], rs_hop.at[48:80], z_bwd)

    project = mm(resid_bf[...], proj[...])
    inverse = lax.rsqrt(jnp.sum(project * project, axis=-1, keepdims=True) + 1e-06)
    unit_f = project * inverse
    embeds = unit_f.astype(BF16)
    eall[0, 0] = embeds
    embeds_first = [send(eall.at[0, 0], eall.at[0, k], shifted(-k)) for k in (1, 2, 3)]

    text_core.wait_recv()
    text_far_core.wait_recv()
    scaling = scale[0]
    offset = bias[0]
    same = lax.broadcasted_iota(jnp.int32, (R, R), 0) == lax.broadcasted_iota(jnp.int32, (R, R), 1)

    def coefs(mine, theirs, q):
        out = []
        for k in range(4):
            logits = scaling * mm_nt(mine, theirs[q, k]) + offset
            soft = jax.nn.sigmoid(logits)
            if q == 0 and k == 0:
                soft = jnp.where(same, -jax.nn.sigmoid(-logits), soft)
            out.append(soft.astype(BF16))
        return out

    def other_side(mine, theirs):
        total = None
        for q in range(4):
            for k, coef in enumerate(coefs(mine, theirs, q)):
                term = mm(coef, theirs[q, k])
                total = term if total is None else total + term
        return scaling * total

    embed_grad = other_side(embeds, tall)
    inner = jnp.sum(unit_f * embed_grad, axis=-1, keepdims=True)
    pd[0, 0] = (inverse * (embed_grad - unit_f * inner)).astype(BF16)
    pd_up = send(pd.at[0, 0], pd.at[0, 3], z_fwd)
    pd_down = send(pd.at[0, 0], pd.at[0, 1], z_bwd)
    pd_core = {0: send(pd.at[0, 0], pd.at[1, 0], core)}
    resid_grad[...] = mm_nt(pd[0, 0], proj[...])
    grad_bf[0, :R, :] = resid_grad[...].astype(BF16)
    pd_core[0].wait_recv()
    grad_bf[0, R:, :] = mm_nt(pd[1, 0], proj[...]).astype(BF16)

    pd_up.wait_recv()
    pd_far_up = send(pd.at[0, 3, :, 0:512], pd.at[0, 2, :, 0:512], z_fwd)
    pd_core[3] = send(pd.at[0, 3], pd.at[1, 3], core)
    pd_down.wait_recv()
    pd_far_down = send(pd.at[0, 1, :, 512:1024], pd.at[0, 2, :, 512:1024], z_bwd)
    pd_core[1] = send(pd.at[0, 1], pd.at[1, 1], core)

    def expand(dz):
        both = jnp.concatenate([pd[0, dz], pd[1, dz]], axis=0)
        grad_bf[dz] = mm_nt(both, proj[...]).astype(BF16)

    for dz in (3, 1):
        pd_core[dz].wait_recv()
        expand(dz)
    pd_far_up.wait_recv()
    pd_far_down.wait_recv()
    pd_core[2] = send(pd.at[0, 2], pd.at[1, 2], core)
    for copy in embeds_first:
        copy.wait_recv()
    embeds_far = send(eall.at[0], eall.at[1], z_far)
    embeds_core = send(eall.at[0], eall.at[2], core)
    rs_hop_up.wait_recv()
    rs_far_up = send(rs_hop.at[0:48], rs.at[0, 2, 0:48], z_fwd)
    rs_hop_down.wait_recv()
    rs_far_down = send(rs_hop.at[48:80], rs.at[0, 2, 48:80], z_bwd)
    pd_core[2].wait_recv()
    expand(2)

    @pl.loop(0, 8)
    def _(p):
        @pl.loop(0, 2)
        def _(i):
            rows = pl.ds(2 * i, 2)
            act_grad = mm_nt(grad_bf[rows].reshape(4 * R, D), dense_out[p])
            pre_grad = (act_grad * slope[p, rows].reshape(4 * R, 2 * U).astype(F32)).astype(BF16)
            for n in range(0, D, 256):
                part = mm(pre_grad, dense_in[p, :, n:n + 256]).reshape(2, 2 * R, 256)

                @pl.when(p == 0)
                def _():
                    acc[rows, :, n:n + 256] = part

                @pl.when(p > 0)
                def _():
                    acc[rows, :, n:n + 256] += part

    rs_up.wait_recv()
    rs_down.wait_recv()
    rs_far_up.wait_recv()
    rs_far_down.wait_recv()
    rs_core = send(rs.at[0], rs.at[1], core)
    embeds_far.wait_recv()
    embeds_far_core = send(eall.at[1], eall.at[3], core)
    pending = reduce_rows(1)
    rs_core.wait_recv()
    columns = pl.ds(pl.multiple_of(mp * 256, 128), 256)
    term = mm_tn(rs[...].reshape(8 * R, H), pd[:, :, :, columns].reshape(8 * R, 256))
    for n in range(16):
        pg[n % 4, n // 4] = term[n * 56:(n + 1) * 56, :].astype(BF16)
    pg_first = [
        send(pg.at[(xi + k) % 4], pg_in.at[k - 1], where)
        for k, where in ((1, x_fwd), (2, x_far), (3, x_bwd))
    ]

    embeds_core.wait_recv()
    embeds_far_core.wait_recv()
    tf, text_inv = text_parts()
    unit_grad = other_side(tall[0, 0], eall)
    text_grad[...] = text_inv * (
        unit_grad - tf * jnp.sum(tf * unit_grad, axis=-1, keepdims=True)
    )

    for copy in pg_first:
        copy.wait_recv()
    part = pg[xi].astype(F32)
    for k in range(3):
        part = part + pg_in[k].astype(F32)
    pg2[...] = part.astype(BF16)
    pg_second = [
        send(pg2.at[(yi + k) % 4], pg2_in.at[k - 1], where)
        for k, where in ((1, y_fwd), (2, y_far), (3, y_bwd))
    ]

    input_grad = reduced(1, pending)
    _, normed, inv_std = norm_rows(own_row)
    scaled = input_grad * gain[...]
    shift = scaled - jnp.mean(scaled, axis=-1, keepdims=True)
    shift = shift - normed * jnp.mean(scaled * normed, axis=-1, keepdims=True)
    d_pooled[...] = resid_grad[...] + inv_std * shift

    for copy in pg_second:
        copy.wait_recv()
    out = pg2[yi].astype(F32)
    for k in range(3):
        out = out + pg2_in[k].astype(F32)
    proj_grad[...] = out

    for copy in started:
        copy.wait_send()


def per_device(pooled, ln_gain, w_in, w_out, proj, text, logit_scale, logit_bias):
    vmem = pl.BlockSpec(memory_space=pltpu.VMEM)
    smem = pl.BlockSpec(memory_space=pltpu.SMEM)
    hbm = pl.BlockSpec(memory_space=pl.ANY)
    return pl.pallas_call(
        kernel,
        out_shape=(
            jax.ShapeDtypeStruct((R, D), F32),
            jax.ShapeDtypeStruct((56, 256), F32),
            jax.ShapeDtypeStruct((R, E), F32),
        ),
        in_specs=[vmem, vmem, hbm, hbm, hbm, vmem, smem, smem],
        out_specs=(vmem, vmem, vmem),
        scratch_shapes=[
            pltpu.VMEM((16, U, D), BF16),
            pltpu.VMEM((16, U, D), BF16),
            pltpu.VMEM((8, 2 * U, D), BF16),
            pltpu.VMEM((8, 2 * U, D), BF16),
            pltpu.VMEM((4, 2 * R, D), BF16),
            pltpu.VMEM((4, 2 * R, D), F32),
            pltpu.VMEM((8, 4, 2 * R, 2 * U), BF16),
            pltpu.VMEM((4, 2 * R, D), BF16),
            pltpu.VMEM((R, D), F32),
            pltpu.VMEM((4, 4, R, E), BF16),
            pltpu.VMEM((4, 4, R, E), BF16),
            pltpu.VMEM((D, E), BF16),
            pltpu.VMEM((2, 4, R, D), BF16),
            pltpu.VMEM((2, 4, R, D), BF16),
            pltpu.VMEM((2, 2, R, H), BF16),
            pltpu.VMEM((2, 2, R, D), BF16),
            pltpu.VMEM((2, 3, R, D), BF16),
            pltpu.VMEM((2, 4, R, E), BF16),
            pltpu.VMEM((R, D), BF16),
            pltpu.VMEM((2, 4, R, H), BF16),
            pltpu.VMEM((R, H), BF16),
            pltpu.VMEM((4, 4, 56, 256), BF16),
            pltpu.VMEM((3, 4, 56, 256), BF16),
            pltpu.VMEM((4, 56, 256), BF16),
            pltpu.VMEM((3, 56, 256), BF16),
            pltpu.SemaphoreType.DMA((N_SEMS,)),
            pltpu.SemaphoreType.DMA((N_SEMS,)),
            pltpu.SemaphoreType.DMA((3,)),
        ],
        compiler_params=pltpu.CompilerParams(
            collective_id=0, has_side_effects=True, vmem_limit_bytes=66 * 1000 * 1000
        ),
    )(pooled, ln_gain.reshape(1, D), w_in, w_out, proj, text, logit_scale, logit_bias)


def solution(mesh):
    in_specs = (
        P("dp", None),
        P(),
        P(("dp", "mp"), None),
        P(("dp", "mp"), None),
        P(),
        P(("dp", "mp"), None),
        P(),
        P(),
    )
    out_specs = (P(("dp", "mp"), None), P("dp", "mp"), P(("dp", "mp"), None))
    return jax.shard_map(
        per_device, mesh=mesh, in_specs=in_specs, out_specs=out_specs, check_vma=False
    )
```

time: 720 us -> 200 us (0.28)
  waiting for transfers between devices: 620 us -> 0 us
  Pallas kernels: 0 us -> 192 us
  matrix products: 65.5 us -> 0 us
  between operations: 15.6 us -> 1.93 us
  other arithmetic: 13.3 us -> 0 us
    all_gather x2 -> x0, waiting for transfers between devices: 332 us -> none  [the longest x1 167 us: per_device(): lax.all_gather(w_in, 'dp', axis=0, tiled=True)]
    pallas_call x0 -> x1, Pallas kernels: none -> 192 us  [per_device(): pl.pallas_call(kernel, out_shape=(jax.ShapeDtypeStruct((R, D), F32), jax....]
    reduce_scatter x2 -> x0, waiting for transfers between devices: 143 us -> none  [the longest x1 88.7 us: per_device(): lax.psum_scatter(proj_term.astype(jnp.bfloat16), 'dp', scatter_dimension=...]
    psum x2 -> x0, waiting for transfers between devices: 105 us -> none  [the longest x1 60.2 us: per_device(): mixed = lax.psum(mixed_part, 'mp')]
    dot_general x18 -> x0, matrix products: 65.5 us -> none  [the longest x1 17.7 us: per_device(): jnp.dot(pre_grad, inputs_all, preferred_element_type=jnp.float32)]
    ppermute x7 -> x0, waiting for transfers between devices: 38.3 us -> none  [from_behind(): return lax.ppermute(block, axis, route)]
  transfers between devices with their start and end apart: 13 -> 0, of which waited for: 11 -> 0; matrix products, arithmetic and copies ran while one was open for 8% -> 0% of each run, Pallas kernels for 0% -> 0%
where the time goes in v1:
time: 200 us
  Pallas kernels  192 us (96%)
  local copies, waits for them, and re-layouts  6.37 us (3%)
    pallas_call x1, Pallas kernels, per_device(): pl.pallas_call(kernel, out_shape=(jax.ShapeDtypeStruct((R, D), F32), jax....  192 us
    unnamed x3, local copies, waits for them, and re-layouts  5.07 us

profile of v1, /device:TPU:1, one launch (start us, length us, event | category | flops | bytes accessed | tf_op | source)
XLA Modules:
  0.0 200.0 jit_solution(928610165589086121)
XLA Ops:
  1.9 1.3 reshape.9.gain
  3.2 191.7 %shard_map.103 = (f32[80,1792]{1,0:T(8,128)}, f32[56,256]{1,0:T(8,128)}, f32[80,1024]{1,0:T(8,128)}) custom-call(bf16[320,1792]{1,0:T(8,128)(2,1)} %pooled.1, f32[1,1792]{1,0:T(1,128)} %reshape.9.gain, bf16[120,1792]{1,0:T(8,128)(2,1)} %w_in.1, bf16[120,1792]{1,0:T(8,128)(2,1)} %w_out.1, bf16[1792,1024]{1,0:T(8,128)(2,1)} %proj_hbm.1, ...), custom_call_target="tpu_custom_call" | custom-call | tf_op jit(solution)/shard_map/pallas_call | solution.py:477
  194.9 1.9 copy.16
  196.8 1.4 copy.17
  198.3 1.7 copy.18

commit v2 on v1

v2 whole, which is shorter than its diff:
```python
import functools

import jax
import jax.numpy as jnp
from jax import lax
from jax.experimental import pallas as pl
from jax.experimental.pallas import tpu as pltpu
from jax.sharding import PartitionSpec as P

D = 1792
H = D // 2
E = 1024
U = 120
R = 80
F32 = jnp.float32
BF16 = jnp.bfloat16
MESH = pl.DeviceIdType.MESH
PAIRS = (
    ((0, 0), (3, 0)),
    ((1, 0), (0, 3)),
    ((0, 1), (3, 3)),
    ((3, 1), (1, 3)),
    ((1, 1), (2, 0)),
    ((0, 2), (2, 3)),
    ((2, 1), (3, 2)),
    ((1, 2), (2, 2)),
)
PLACE = {0: 0, 1: 1, 3: 2, 2: 3}
N_SEMS = 128


def mm(a, b):
    return lax.dot_general(a, b, (((1,), (0,)), ((), ())), preferred_element_type=F32)


def mm_nt(a, b):
    return lax.dot_general(a, b, (((1,), (1,)), ((), ())), preferred_element_type=F32)


def mm_tn(a, b):
    return lax.dot_general(a, b, (((0,), (0,)), ((), ())), preferred_element_type=F32)


def gelu_and_slope(v):
    c = 0.7978845608028654
    v2 = v * v
    t = jnp.tanh(c * v * (1.0 + 0.044715 * v2))
    half = 0.5 * (1.0 + t)
    act = v * half
    slope = half + (0.5 * v) * (1.0 - t * t) * (c * (1.0 + 3.0 * 0.044715 * v2))
    return act, slope


def kernel(
    pooled, gain, w_in, w_out, proj_hbm, text, scale, bias,
    d_pooled, proj_grad, text_grad,
    slot_in, slot_out, dense_in, dense_out, x, acc, slope, resid_grad,
    tall, eall, proj, stage, core_in, hop, fin, direct, pd, resid_bf, rs, unit_part,
    pg, pg_in, pg2, pg2_in, send_sems, recv_sems, local_sems,
):
    dp = lax.axis_index("dp")
    mp = lax.axis_index("mp")
    z_lo = dp // 16
    yi = (dp // 4) % 4
    xi = dp % 4
    z_hi = mp // 2
    c = mp % 2
    z = z_hi * 2 + z_lo

    def place(dx=0, dy=0, dz=0, other=False):
        nz = (z + dz) % 4
        ndp = (nz % 2) * 16 + ((yi + dy) % 4) * 4 + (xi + dx) % 4
        nmp = (nz // 2) * 2 + (1 - c if other else c)
        return {"dp": ndp, "mp": nmp}

    def shifted(k):
        return {"dp": (dp + k + 32) % 32, "mp": mp}

    along_x = {k: place(dx=k) for k in (3, 1, 2)}
    along_y = {k: place(dy=k) for k in (3, 1, 2)}
    z_fwd, z_bwd, z_far = place(dz=1), place(dz=3), place(dz=2)
    core = place(other=True)

    count = [0]
    started = []

    def send(src, dst, where):
        n = count[0]
        count[0] += 1
        copy = pltpu.make_async_remote_copy(
            src_ref=src, dst_ref=dst, send_sem=send_sems.at[n], recv_sem=recv_sems.at[n],
            device_id=where, device_id_type=MESH,
        )
        copy.start()
        started.append(copy)
        return copy

    def sent(copies):
        for copy in copies:
            copy.wait_send()
            started[:] = [other for other in started if other is not copy]

    def arrived(copies):
        for copy in copies:
            copy.wait_recv()

    def slot(dx, dy):
        return dy * 4 + dx

    locals_ = [
        pltpu.make_async_copy(w_in, slot_in.at[0], local_sems.at[0]),
        pltpu.make_async_copy(w_out, slot_out.at[0], local_sems.at[1]),
        pltpu.make_async_copy(proj_hbm, proj, local_sems.at[2]),
    ]
    for copy in locals_:
        copy.start()

    peers = list(along_x.values()) + list(along_y.values()) + [z_fwd, z_bwd, z_far, core]
    peers += [shifted(k) for k in (-3, -2, -1, 1, 2, 3)]
    barrier = pltpu.get_barrier_semaphore()
    for peer in peers:
        pl.semaphore_signal(barrier, inc=1, device_id=peer, device_id_type=MESH)
    pl.semaphore_wait(barrier, len(peers))

    arrive = {}

    def give(which, src, at, where, half=None):
        target = (slot_in if which == "in" else slot_out).at[slot(*at)]
        if half is not None:
            columns = pl.ds(half * H, H)
            target, src = target.at[:, columns], src.at[:, columns]
        arrive[which, at, half] = send(src, target, where)

    def held(which, at):
        return (slot_in if which == "in" else slot_out).at[slot(*at)]

    def got(which, at, half=None):
        arrive[which, at, half].wait_recv()

    def got_halves(which, at):
        got(which, at, 0)
        got(which, at, 1)

    def give_both_ways(which, at, axis, src=None):
        src = held(which, at) if src is None else src
        if axis == "x":
            give(which, src, ((at[0] + 3) % 4, at[1]), along_x[1])
            give(which, src, ((at[0] + 1) % 4, at[1]), along_x[3])
        else:
            give(which, src, (at[0], (at[1] + 3) % 4), along_y[1])
            give(which, src, (at[0], (at[1] + 1) % 4), along_y[3])

    def pass_on(which, at, axis):
        dx, dy = at
        src = held(which, at)
        if axis == "x":
            k, half = (1, 0) if dx == 3 else (3, 1)
            give(which, src, (2, dy), along_x[k], half)
        else:
            k, half = (1, 0) if dy == 3 else (3, 1)
            give(which, src, (dx, 2), along_y[k], half)

    give_both_ways("in", (0, 0), "x", w_in)
    give_both_ways("out", (0, 0), "y", w_out)
    give_both_ways("out", (0, 0), "x", w_out)
    give_both_ways("in", (0, 0), "y", w_in)

    def norm_rows(start):
        h = pooled[pl.ds(pl.multiple_of(start, 16), R), :].astype(F32)
        center = h - jnp.mean(h, axis=-1, keepdims=True)
        inv_std = lax.rsqrt(jnp.mean(center * center, axis=-1, keepdims=True) + 1e-06)
        return h, center * inv_std, inv_std

    own_row = z_hi * 160 + c * R
    other_row = z_hi * 160 + (1 - c) * R
    far_own = (1 - z_hi) * 160 + c * R
    far_other = (1 - z_hi) * 160 + (1 - c) * R

    def fill_x(dz, j, start):
        x[PLACE[dz], j * R:(j + 1) * R, :] = (norm_rows(start)[1] * gain[...]).astype(BF16)

    fill_x(0, 0, own_row)
    fill_x(0, 1, other_row)
    x_up = send(x.at[PLACE[0]], x.at[PLACE[3]], z_fwd)
    x_down = send(x.at[PLACE[0]], x.at[PLACE[1]], z_bwd)

    def text_parts():
        t = text[...].astype(F32)
        inv = lax.rsqrt(jnp.sum(t * t, axis=-1, keepdims=True) + 1e-06)
        return t * inv, inv

    tall[0, 0] = text_parts()[0].astype(BF16)
    text_far = send(tall.at[0, 0], tall.at[1, 0], z_far)
    fill_x(2, 0, far_own)
    fill_x(2, 1, far_other)

    def forward_pair(p):
        s0, s1 = slot(*PAIRS[p][0]), slot(*PAIRS[p][1])
        for ref, dense in ((slot_in, dense_in), (slot_out, dense_out)):
            both = jnp.concatenate([ref[s0].astype(F32), ref[s1].astype(F32)], axis=0)
            dense[p] = both.astype(BF16)
        pre = mm_nt(x[...].reshape(8 * R, D), dense_in[p])
        act, der = gelu_and_slope(pre)
        slope[p] = der.astype(BF16).reshape(4, 2 * R, 2 * U)
        act = act.astype(BF16)
        for n in range(0, D, 256):
            part = mm(act, dense_out[p, :, n:n + 256]).reshape(4, 2 * R, 256)
            if p == 0:
                acc[:, :, n:n + 256] = part
            else:
                acc[:, :, n:n + 256] += part

    for copy in locals_:
        copy.wait()
    for k in (3, 1):
        got("in", (k, 0))
        pass_on("in", (k, 0), "x")
        got("out", (0, k))
        pass_on("out", (0, k), "y")
    for k in (3, 1):
        give_both_ways("in", (k, 0), "y")
        give_both_ways("out", (0, k), "x")
    for k in (3, 1):
        got("in", (0, k))
        pass_on("in", (0, k), "y")
        got("out", (k, 0))
        pass_on("out", (k, 0), "x")
    arrived([x_up, x_down])
    sent([x_up, x_down])
    text_far.wait_recv()
    text_core = [send(tall.at[0:2, 0], tall.at[2:4, 0], core)]
    forward_pair(0)
    got_halves("in", (2, 0))
    give_both_ways("in", (2, 0), "y")
    got_halves("out", (0, 2))
    give_both_ways("out", (0, 2), "x")
    forward_pair(1)
    for j in (3, 1):
        for k in (3, 1):
            got("in", (j, k))
            pass_on("in", (j, k), "y")
            got("out", (k, j))
            pass_on("out", (k, j), "x")
    forward_pair(2)
    forward_pair(3)
    got_halves("in", (0, 2))
    got_halves("out", (2, 0))
    for k in (3, 1):
        got("in", (2, k))
        pass_on("in", (2, k), "y")
        got("out", (k, 2))
        pass_on("out", (k, 2), "x")
    forward_pair(4)
    got_halves("out", (2, 3))
    forward_pair(5)
    got_halves("out", (2, 1))
    got_halves("in", (3, 2))
    forward_pair(6)
    got_halves("in", (1, 2))
    got_halves("in", (2, 2))
    got_halves("out", (2, 2))
    text_next = [send(tall.at[0:2, 0], tall.at[0:2, k], shifted(k)) for k in (1, 3, 2)]
    forward_pair(7)

    lo, hi = slice(0, H), slice(H, D)
    own, other = slice(0, R), slice(R, 2 * R)

    class Rows:
        def __init__(self, turn):
            self.turn = turn
            self.core = {}
            self.last = []

        def offer(self, dz):
            stage[dz] = acc[PLACE[dz], other, :].astype(BF16)
            self.core[dz] = send(stage.at[dz], core_in.at[self.turn, dz], core)

        def both(self, dz, columns):
            theirs = core_in[self.turn, dz, :, columns].astype(F32)
            return acc[PLACE[dz], own, columns] + theirs

        def far(self):
            turn = self.turn
            self.core[2].wait_recv()
            direct[0] = self.both(2, slice(0, D)).astype(BF16)
            self.up = send(direct.at[0, :, lo], hop.at[turn, 0], z_fwd)
            self.down = send(direct.at[0, :, hi], hop.at[turn, 1], z_bwd)

        def near_up(self):
            turn = self.turn
            self.core[1].wait_recv()
            direct[1, :, hi] = self.both(1, hi).astype(BF16)
            self.last.append(send(direct.at[1, :, hi], fin.at[turn, 0, :, hi], z_fwd))

        def near_down(self):
            turn = self.turn
            self.core[3].wait_recv()
            direct[2, :, lo] = self.both(3, lo).astype(BF16)
            self.last.append(send(direct.at[2, :, lo], fin.at[turn, 1, :, lo], z_bwd))

        def hops(self):
            turn = self.turn
            self.up.wait_recv()
            total = self.both(1, lo) + hop[turn, 0].astype(F32)
            direct[1, :, lo] = total.astype(BF16)
            self.last.append(send(direct.at[1, :, lo], fin.at[turn, 0, :, lo], z_fwd))
            self.down.wait_recv()
            total = self.both(3, hi) + hop[turn, 1].astype(F32)
            direct[2, :, hi] = total.astype(BF16)
            self.last.append(send(direct.at[2, :, hi], fin.at[turn, 1, :, hi], z_bwd))

        def result(self):
            turn = self.turn
            self.core[0].wait_recv()
            mine = self.both(0, slice(0, D))
            arrived(self.last)
            return mine + fin[turn, 0].astype(F32) + fin[turn, 1].astype(F32)

    rows = Rows(0)
    for dz in (2, 1, 3, 0):
        rows.offer(dz)
    rows.far()
    rows.near_up()
    rows.near_down()
    rows.hops()
    mixed = rows.result()
    pooled_rows = pooled[pl.ds(pl.multiple_of(own_row, 16), R), :].astype(F32)
    resid_bf[...] = (pooled_rows + mixed).astype(BF16)

    own_cols = pl.ds(pl.multiple_of(z_lo * H, 128), H)
    other_cols = pl.ds(pl.multiple_of((1 - z_lo) * H, 128), H)
    project = mm(resid_bf[...], proj[...])
    inverse = lax.rsqrt(jnp.sum(project * project, axis=-1, keepdims=True) + 1e-06)
    unit_f = project * inverse
    embeds = unit_f.astype(BF16)
    eall[0, 0] = embeds
    embeds_first = [send(eall.at[0, 0], eall.at[0, k], shifted(-k)) for k in (1, 2, 3)]

    for n, k in enumerate((1, 3, 2)):
        text_next[n].wait_recv()
        text_core.append(send(tall.at[0:2, k], tall.at[2:4, k], core))
    arrived(text_core)
    scaling = scale[0]
    offset = bias[0]
    same = lax.broadcasted_iota(jnp.int32, (R, R), 0) == lax.broadcasted_iota(jnp.int32, (R, R), 1)

    def other_side(mine, theirs, slabs, positive):
        total = None
        for n in range(4 * slabs):
            block = theirs[n // 4, n % 4]
            logits = scaling * mm_nt(mine, block) + offset
            soft = jax.nn.sigmoid(logits)
            if positive and n == 0:
                soft = jnp.where(same, -jax.nn.sigmoid(-logits), soft)
            term = mm(soft.astype(BF16), block)
            total = term if total is None else total + term
        return scaling * total

    grad_bf = x
    embed_grad = other_side(embeds, tall, 4, True)
    inner = jnp.sum(unit_f * embed_grad, axis=-1, keepdims=True)
    pd[0, 0] = (inverse * (embed_grad - unit_f * inner)).astype(BF16)
    pd_up = send(pd.at[0, 0], pd.at[0, PLACE[3]], z_fwd)
    pd_down = send(pd.at[0, 0], pd.at[0, PLACE[1]], z_bwd)
    pd_core = {0: send(pd.at[0, 0], pd.at[1, 0], core)}
    resid_grad[...] = mm_nt(pd[0, 0], proj[...])
    grad_bf[0, own, :] = resid_grad[...].astype(BF16)
    pd_core[0].wait_recv()
    grad_bf[0, other, :] = mm_nt(pd[1, 0], proj[...]).astype(BF16)

    def expand(first, last):
        both = pd[0:2, first:last]
        pieces = [both[j, n] for n in range(last - first) for j in range(2)]
        grads = mm_nt(jnp.concatenate(pieces, axis=0), proj[...])
        grad_bf[first:last] = grads.astype(BF16).reshape(last - first, 2 * R, D)

    def hidden_back(first, last):
        n = (last - first) * 2 * R
        for p in range(8):
            act_grad = mm_nt(grad_bf[first:last].reshape(n, D), dense_out[p])
            der = slope[p, first:last].reshape(n, 2 * U).astype(F32)
            slope[p, first:last] = (act_grad * der).astype(BF16).reshape(last - first, 2 * R, 2 * U)

    def input_back(dz):
        at = PLACE[dz]
        for n in range(0, D, 256):
            total = mm(slope[0, at], dense_in[0, :, n:n + 256])
            for p in range(1, 8):
                total = total + mm(slope[p, at], dense_in[p, :, n:n + 256])
            acc[at, :, n:n + 256] = total

    def pass_delta(dz):
        at = PLACE[dz]
        half, where = (pl.ds(0, E // 2), z_fwd) if dz == 3 else (pl.ds(E // 2, E // 2), z_bwd)
        on = send(pd.at[0, at, :, half], pd.at[0, PLACE[2], :, half], where)
        pd_core[dz] = send(pd.at[0, at], pd.at[1, at], core)
        return on

    hidden_back(0, 1)
    pd_up.wait_recv()
    pd_far = [pass_delta(3)]
    pd_down.wait_recv()
    pd_far.append(pass_delta(1))
    rs[0, 0] = resid_bf[:, own_cols]
    rs_in = [
        send(resid_bf.at[:, other_cols], rs.at[0, PLACE[3]], z_fwd),
        send(resid_bf.at[:, other_cols], rs.at[0, PLACE[1]], z_bwd),
        send(resid_bf.at[:, own_cols], rs.at[0, PLACE[2]], z_far),
    ]
    arrived(embeds_first)
    embeds_core = send(eall.at[0], eall.at[1], core)
    arrived([pd_core[3], pd_core[1]])
    expand(1, 3)
    arrived(pd_far)
    pd_core[2] = send(pd.at[0, PLACE[2]], pd.at[1, PLACE[2]], core)
    hidden_back(1, 3)
    embeds_core.wait_recv()
    unit_part[0] = other_side(tall[1, 0], eall, 2, False).astype(BF16)
    unit_far = send(unit_part.at[0], unit_part.at[1], z_far)
    pd_core[2].wait_recv()
    expand(3, 4)
    hidden_back(3, 4)

    sent(list(rows.core.values()) + rows.last + [rows.up, rows.down])
    rows = Rows(1)
    input_back(2)
    rows.offer(2)
    arrived(rs_in)
    rs_core = send(rs.at[0], rs.at[1], core)
    input_back(1)
    rows.offer(1)
    rows.far()
    input_back(3)
    rows.offer(3)
    rows.near_up()
    rows.near_down()

    rs_core.wait_recv()
    columns = pl.ds(pl.multiple_of(mp * 256, 128), 256)
    term = mm_tn(rs[...].reshape(8 * R, H), pd[:, :, :, columns].reshape(8 * R, 256))
    for n in range(16):
        pg[n % 4, n // 4] = term[n * 56:(n + 1) * 56, :].astype(BF16)
    pg_first = [send(pg.at[(xi + k) % 4], pg_in.at[k - 1], along_x[k]) for k in (1, 2, 3)]
    rows.hops()
    input_back(0)
    rows.offer(0)

    tf, text_inv = text_parts()
    unit_grad = other_side(tall[0, 0], eall, 2, True)
    unit_far.wait_recv()
    unit_grad = unit_grad + unit_part[1].astype(F32)
    text_grad[...] = text_inv * (
        unit_grad - tf * jnp.sum(tf * unit_grad, axis=-1, keepdims=True)
    )

    arrived(pg_first)
    part = pg[xi].astype(F32)
    for k in range(3):
        part = part + pg_in[k].astype(F32)
    pg2[...] = part.astype(BF16)
    pg_second = [send(pg2.at[(yi + k) % 4], pg2_in.at[k - 1], along_y[k]) for k in (1, 2, 3)]

    input_grad = rows.result()
    _, normed, inv_std = norm_rows(own_row)
    scaled = input_grad * gain[...]
    shift = scaled - jnp.mean(scaled, axis=-1, keepdims=True)
    shift = shift - normed * jnp.mean(scaled * normed, axis=-1, keepdims=True)
    d_pooled[...] = resid_grad[...] + inv_std * shift

    arrived(pg_second)
    out = pg2[yi].astype(F32)
    for k in range(3):
        out = out + pg2_in[k].astype(F32)
    proj_grad[...] = out

    for copy in started:
        copy.wait_send()


def per_device(pooled, ln_gain, w_in, w_out, proj, text, logit_scale, logit_bias):
    vmem = pl.BlockSpec(memory_space=pltpu.VMEM)
    smem = pl.BlockSpec(memory_space=pltpu.SMEM)
    hbm = pl.BlockSpec(memory_space=pl.ANY)
    return pl.pallas_call(
        kernel,
        out_shape=(
            jax.ShapeDtypeStruct((R, D), F32),
            jax.ShapeDtypeStruct((56, 256), F32),
            jax.ShapeDtypeStruct((R, E), F32),
        ),
        in_specs=[vmem, vmem, hbm, hbm, hbm, vmem, smem, smem],
        out_specs=(vmem, vmem, vmem),
        scratch_shapes=[
            pltpu.VMEM((16, U, D), BF16),
            pltpu.VMEM((16, U, D), BF16),
            pltpu.VMEM((8, 2 * U, D), BF16),
            pltpu.VMEM((8, 2 * U, D), BF16),
            pltpu.VMEM((4, 2 * R, D), BF16),
            pltpu.VMEM((4, 2 * R, D), F32),
            pltpu.VMEM((8, 4, 2 * R, 2 * U), BF16),
            pltpu.VMEM((R, D), F32),
            pltpu.VMEM((4, 4, R, E), BF16),
            pltpu.VMEM((2, 4, R, E), BF16),
            pltpu.VMEM((D, E), BF16),
            pltpu.VMEM((4, R, D), BF16),
            pltpu.VMEM((2, 4, R, D), BF16),
            pltpu.VMEM((2, 2, R, H), BF16),
            pltpu.VMEM((2, 2, R, D), BF16),
            pltpu.VMEM((3, R, D), BF16),
            pltpu.VMEM((2, 4, R, E), BF16),
            pltpu.VMEM((R, D), BF16),
            pltpu.VMEM((2, 4, R, H), BF16),
            pltpu.VMEM((2, R, E), BF16),
            pltpu.VMEM((4, 4, 56, 256), BF16),
            pltpu.VMEM((3, 4, 56, 256), BF16),
            pltpu.VMEM((4, 56, 256), BF16),
            pltpu.VMEM((3, 56, 256), BF16),
            pltpu.SemaphoreType.DMA((N_SEMS,)),
            pltpu.SemaphoreType.DMA((N_SEMS,)),
            pltpu.SemaphoreType.DMA((3,)),
        ],
        compiler_params=pltpu.CompilerParams(
            collective_id=0, has_side_effects=True, vmem_limit_bytes=64 * 1024 * 1024
        ),
    )(pooled, ln_gain.reshape(1, D), w_in, w_out, proj, text, logit_scale, logit_bias)


def solution(mesh):
    in_specs = (
        P("dp", None),
        P(),
        P(("dp", "mp"), None),
        P(("dp", "mp"), None),
        P(),
        P(("dp", "mp"), None),
        P(),
        P(),
    )
    out_specs = (P(("dp", "mp"), None), P("dp", "mp"), P(("dp", "mp"), None))
    return jax.shard_map(
        per_device, mesh=mesh, in_specs=in_specs, out_specs=out_specs, check_vma=False
    )
```

time: 200 us -> 166 us (0.83)
  Pallas kernels: 192 us -> 158 us
    pallas_call x1, Pallas kernels: 192 us -> 158 us  [per_device(): pl.pallas_call(kernel, out_shape=(jax.ShapeDtypeStruct((R, D), F32), jax....]
where the time goes in v2:
time: 166 us
  Pallas kernels  158 us (95%)
  local copies, waits for them, and re-layouts  6.37 us (4%)
  between operations  1.93 us (1%)
    pallas_call x1, Pallas kernels, per_device(): pl.pallas_call(kernel, out_shape=(jax.ShapeDtypeStruct((R, D), F32), jax....  158 us
    unnamed x3, local copies, waits for them, and re-layouts  5.07 us

profile of v2, /device:TPU:1, one launch (start us, length us, event | category | flops | bytes accessed | tf_op | source)
XLA Modules:
  0.0 165.9 jit_solution(11280053242190707117)
XLA Ops:
  1.9 1.3 reshape.9.gain
  3.2 157.6 %shard_map.103 = (f32[80,1792]{1,0:T(8,128)}, f32[56,256]{1,0:T(8,128)}, f32[80,1024]{1,0:T(8,128)}) custom-call(bf16[320,1792]{1,0:T(8,128)(2,1)} %pooled.1, f32[1,1792]{1,0:T(1,128)} %reshape.9.gain, bf16[120,1792]{1,0:T(8,128)(2,1)} %w_in.1, bf16[120,1792]{1,0:T(8,128)(2,1)} %w_out.1, bf16[1792,1024]{1,0:T(8,128)(2,1)} %proj_hbm.1, ...), custom_call_target="tpu_custom_call" | custom-call | tf_op jit(solution)/shard_map/pallas_call | solution.py:484
  160.8 1.9 %copy.16 = f32[80,1792]{1,0:T(8,128)} copy(f32[80,1792]{1,0:T(8,128)} %get-tuple-element.6) | data formatting | bytes 1146880
  162.7 1.4 copy.17
  164.2 1.7 %copy.18 = f32[80,1024]{1,0:T(8,128)} copy(f32[80,1024]{1,0:T(8,128)} %get-tuple-element.8) | data formatting | bytes 655360

commit v3 on v2

--- a/solution.py
+++ b/solution.py
@@ -177,7 +177,7 @@
     far_other = (1 - z_hi) * 160 + (1 - c) * R
 
     def fill_x(dz, j, start):
-        x[PLACE[dz], j * R:(j + 1) * R, :] = (norm_rows(start)[1] * gain[...]).astype(BF16)
+        x[PLACE[dz], j * R:(j + 1) * R, :] = (norm_rows(start)[1] * gain[...].reshape(1, D)).astype(BF16)
 
     fill_x(0, 0, own_row)
     fill_x(0, 1, other_row)
@@ -190,7 +190,7 @@
         return t * inv, inv
 
     tall[0, 0] = text_parts()[0].astype(BF16)
-    text_far = send(tall.at[0, 0], tall.at[1, 0], z_far)
+    text_first = [send(tall.at[0, 0], tall.at[0, k], shifted(k)) for k in (1, 2, 3)]
     fill_x(2, 0, far_own)
     fill_x(2, 1, far_other)
 
@@ -227,8 +227,9 @@
         pass_on("out", (k, 0), "x")
     arrived([x_up, x_down])
     sent([x_up, x_down])
-    text_far.wait_recv()
-    text_core = [send(tall.at[0:2, 0], tall.at[2:4, 0], core)]
+    arrived(text_first)
+    text_far = send(tall.at[0], tall.at[1], z_far)
+    text_core = [send(tall.at[0], tall.at[2], core)]
     forward_pair(0)
     got_halves("in", (2, 0))
     give_both_ways("in", (2, 0), "y")
@@ -242,6 +243,8 @@
             got("out", (k, j))
             pass_on("out", (k, j), "x")
     forward_pair(2)
+    text_far.wait_recv()
+    text_core.append(send(tall.at[1], tall.at[3], core))
     forward_pair(3)
     got_halves("in", (0, 2))
     got_halves("out", (2, 0))
@@ -259,7 +262,6 @@
     got_halves("in", (1, 2))
     got_halves("in", (2, 2))
     got_halves("out", (2, 2))
-    text_next = [send(tall.at[0:2, 0], tall.at[0:2, k], shifted(k)) for k in (1, 3, 2)]
     forward_pair(7)
 
     lo, hi = slice(0, H), slice(H, D)
@@ -329,16 +331,19 @@
 
     own_cols = pl.ds(pl.multiple_of(z_lo * H, 128), H)
     other_cols = pl.ds(pl.multiple_of((1 - z_lo) * H, 128), H)
+    rs[0, 0] = resid_bf[:, own_cols]
+    rs_in = [
+        send(resid_bf.at[:, other_cols], rs.at[0, PLACE[3]], z_fwd),
+        send(resid_bf.at[:, other_cols], rs.at[0, PLACE[1]], z_bwd),
+        send(resid_bf.at[:, own_cols], rs.at[0, PLACE[2]], z_far),
+    ]
+
     project = mm(resid_bf[...], proj[...])
     inverse = lax.rsqrt(jnp.sum(project * project, axis=-1, keepdims=True) + 1e-06)
     unit_f = project * inverse
     embeds = unit_f.astype(BF16)
     eall[0, 0] = embeds
-    embeds_first = [send(eall.at[0, 0], eall.at[0, k], shifted(-k)) for k in (1, 2, 3)]
-
-    for n, k in enumerate((1, 3, 2)):
-        text_next[n].wait_recv()
-        text_core.append(send(tall.at[0:2, k], tall.at[2:4, k], core))
+
     arrived(text_core)
     scaling = scale[0]
     offset = bias[0]
@@ -401,22 +406,12 @@
     pd_far = [pass_delta(3)]
     pd_down.wait_recv()
     pd_far.append(pass_delta(1))
-    rs[0, 0] = resid_bf[:, own_cols]
-    rs_in = [
-        send(resid_bf.at[:, other_cols], rs.at[0, PLACE[3]], z_fwd),
-        send(resid_bf.at[:, other_cols], rs.at[0, PLACE[1]], z_bwd),
-        send(resid_bf.at[:, own_cols], rs.at[0, PLACE[2]], z_far),
-    ]
-    arrived(embeds_first)
-    embeds_core = send(eall.at[0], eall.at[1], core)
+    embeds_first = [send(eall.at[0, 0], eall.at[0, k], shifted(-k)) for k in (1, 2, 3)]
     arrived([pd_core[3], pd_core[1]])
     expand(1, 3)
     arrived(pd_far)
     pd_core[2] = send(pd.at[0, PLACE[2]], pd.at[1, PLACE[2]], core)
     hidden_back(1, 3)
-    embeds_core.wait_recv()
-    unit_part[0] = other_side(tall[1, 0], eall, 2, False).astype(BF16)
-    unit_far = send(unit_part.at[0], unit_part.at[1], z_far)
     pd_core[2].wait_recv()
     expand(3, 4)
     hidden_back(3, 4)
@@ -427,6 +422,8 @@
     rows.offer(2)
     arrived(rs_in)
     rs_core = send(rs.at[0], rs.at[1], core)
+    arrived(embeds_first)
+    embeds_core = send(eall.at[0], eall.at[1], core)
     input_back(1)
     rows.offer(1)
     rows.far()
@@ -442,16 +439,11 @@
         pg[n % 4, n // 4] = term[n * 56:(n + 1) * 56, :].astype(BF16)
     pg_first = [send(pg.at[(xi + k) % 4], pg_in.at[k - 1], along_x[k]) for k in (1, 2, 3)]
     rows.hops()
+    embeds_core.wait_recv()
+    unit_part[0] = other_side(tall[1, 0], eall, 2, False).astype(BF16)
+    unit_far = send(unit_part.at[0], unit_part.at[1], z_far)
     input_back(0)
     rows.offer(0)
-
-    tf, text_inv = text_parts()
-    unit_grad = other_side(tall[0, 0], eall, 2, True)
-    unit_far.wait_recv()
-    unit_grad = unit_grad + unit_part[1].astype(F32)
-    text_grad[...] = text_inv * (
-        unit_grad - tf * jnp.sum(tf * unit_grad, axis=-1, keepdims=True)
-    )
 
     arrived(pg_first)
     part = pg[xi].astype(F32)
@@ -460,12 +452,20 @@
     pg2[...] = part.astype(BF16)
     pg_second = [send(pg2.at[(yi + k) % 4], pg2_in.at[k - 1], along_y[k]) for k in (1, 2, 3)]
 
+    tf, text_inv = text_parts()
+    unit_grad = other_side(tall[0, 0], eall, 2, True)
     input_grad = rows.result()
     _, normed, inv_std = norm_rows(own_row)
-    scaled = input_grad * gain[...]
+    scaled = input_grad * gain[...].reshape(1, D)
     shift = scaled - jnp.mean(scaled, axis=-1, keepdims=True)
     shift = shift - normed * jnp.mean(scaled * normed, axis=-1, keepdims=True)
     d_pooled[...] = resid_grad[...] + inv_std * shift
+
+    unit_far.wait_recv()
+    unit_grad = unit_grad + unit_part[1].astype(F32)
+    text_grad[...] = text_inv * (
+        unit_grad - tf * jnp.sum(tf * unit_grad, axis=-1, keepdims=True)
+    )
 
     arrived(pg_second)
     out = pg2[yi].astype(F32)
@@ -477,11 +477,17 @@
         copy.wait_send()
 
 
+def write_out(d_in, p_in, t_in, d_out, p_out, t_out):
+    d_out[...] = d_in[...]
+    p_out[...] = p_in[...]
+    t_out[...] = t_in[...]
+
+
 def per_device(pooled, ln_gain, w_in, w_out, proj, text, logit_scale, logit_bias):
     vmem = pl.BlockSpec(memory_space=pltpu.VMEM)
     smem = pl.BlockSpec(memory_space=pltpu.SMEM)
     hbm = pl.BlockSpec(memory_space=pl.ANY)
-    return pl.pallas_call(
+    results = pl.pallas_call(
         kernel,
         out_shape=(
             jax.ShapeDtypeStruct((R, D), F32),
@@ -522,7 +528,13 @@
         compiler_params=pltpu.CompilerParams(
             collective_id=0, has_side_effects=True, vmem_limit_bytes=64 * 1024 * 1024
         ),
-    )(pooled, ln_gain.reshape(1, D), w_in, w_out, proj, text, logit_scale, logit_bias)
+    )(pooled, ln_gain, w_in, w_out, proj, text, logit_scale, logit_bias)
+    return pl.pallas_call(
+        write_out,
+        out_shape=[jax.ShapeDtypeStruct(r.shape, r.dtype) for r in results],
+        in_specs=[vmem] * 3,
+        out_specs=[vmem] * 3,
+    )(*results)
 
 
 def solution(mesh):

time: 166 us -> 155 us (0.934)
  local copies, waits for them, and re-layouts: 6.37 us -> 0 us
  Pallas kernels: 158 us -> 153 us
    pallas_call x1, Pallas kernels: 158 us -> 151 us  [per_device(): pl.pallas_call(kernel, out_shape=(jax.ShapeDtypeStruct((R, D), F32), jax....]
    unnamed x3 -> x0, local copies, waits for them, and re-layouts: 5.07 us -> none
    pallas_call x0 -> x1, Pallas kernels: none -> 2.14 us  [per_device(): pl.pallas_call(write_out, out_shape=[jax.ShapeDtypeStruct(r.shape, r.dtyp...]
where the time goes in v3:
time: 155 us
  Pallas kernels  153 us (99%)
  between operations  1.93 us (1%)
    pallas_call x1, Pallas kernels, per_device(): pl.pallas_call(kernel, out_shape=(jax.ShapeDtypeStruct((R, D), F32), jax....  151 us

profile of v3, /device:TPU:1, one launch (start us, length us, event | category | flops | bytes accessed | tf_op | source)
XLA Modules:
  0.0 154.7 jit_solution(4148479241053428816)
XLA Ops:
  1.9 150.6 %shard_map.103 = (f32[80,1792]{1,0:T(8,128)}, f32[56,256]{1,0:T(8,128)}, f32[80,1024]{1,0:T(8,128)}) custom-call(bf16[320,1792]{1,0:T(8,128)(2,1)} %pooled.1, f32[1792]{0:T(1024)} %gain.1, bf16[120,1792]{1,0:T(8,128)(2,1)} %w_in.1, bf16[120,1792]{1,0:T(8,128)(2,1)} %w_out.1, bf16[1792,1024]{1,0:T(8,128)(2,1)} %proj_hbm.1, bf16[80,1024]{1,0:T(8,128)(2,1)} %text.1, ...), custom_call_target="tpu_custom_call" | custom-call | tf_op jit(solution)/shard_map/pallas_call | solution.py:490
  152.5 2.1 %shard_map.104 = (f32[80,1792]{1,0:T(8,128)}, f32[56,256]{1,0:T(8,128)}, f32[80,1024]{1,0:T(8,128)}) custom-call(f32[80,1792]{1,0:T(8,128)} %get-tuple-element.6.d_in, f32[56,256]{1,0:T(8,128)} %get-tuple-element.7.p_in, f32[80,1024]{1,0:T(8,128)} %get-tuple-element.8.t_in), custom_call_target="tpu_custom_call" | custom-call | tf_op jit(solution)/shard_map/pallas_call | solution.py:532

commit v4 on v3

--- a/solution.py
+++ b/solution.py
@@ -194,6 +194,62 @@
     fill_x(2, 0, far_own)
     fill_x(2, 1, far_other)
 
+    lo, hi = slice(0, H), slice(H, D)
+    own, other = slice(0, R), slice(R, 2 * R)
+
+    class Rows:
+        def __init__(self, turn):
+            self.turn = turn
+            self.core = {}
+            self.last = []
+
+        def offer(self, dz):
+            stage[dz] = acc[PLACE[dz], other, :].astype(BF16)
+            self.core[dz] = send(stage.at[dz], core_in.at[self.turn, dz], core)
+
+        def both(self, dz, columns):
+            theirs = core_in[self.turn, dz, :, columns].astype(F32)
+            return acc[PLACE[dz], own, columns] + theirs
+
+        def far(self):
+            turn = self.turn
+            self.core[2].wait_recv()
+            direct[0] = self.both(2, slice(0, D)).astype(BF16)
+            self.up = send(direct.at[0, :, lo], hop.at[turn, 0], z_fwd)
+            self.down = send(direct.at[0, :, hi], hop.at[turn, 1], z_bwd)
+
+        def near_up(self):
+            turn = self.turn
+            self.core[1].wait_recv()
+            direct[1, :, hi] = self.both(1, hi).astype(BF16)
+            self.last.append(send(direct.at[1, :, hi], fin.at[turn, 0, :, hi], z_fwd))
+
+        def near_down(self):
+            turn = self.turn
+            self.core[3].wait_recv()
+            direct[2, :, lo] = self.both(3, lo).astype(BF16)
+            self.last.append(send(direct.at[2, :, lo], fin.at[turn, 1, :, lo], z_bwd))
+
+        def hops(self):
+            turn = self.turn
+            self.up.wait_recv()
+            total = self.both(1, lo) + hop[turn, 0].astype(F32)
+            direct[1, :, lo] = total.astype(BF16)
+            self.last.append(send(direct.at[1, :, lo], fin.at[turn, 0, :, lo], z_fwd))
+            self.down.wait_recv()
+            total = self.both(3, hi) + hop[turn, 1].astype(F32)
+            direct[2, :, hi] = total.astype(BF16)
+            self.last.append(send(direct.at[2, :, hi], fin.at[turn, 1, :, hi], z_bwd))
+
+        def result(self):
+            turn = self.turn
+            self.core[0].wait_recv()
+            mine = self.both(0, slice(0, D))
+            arrived(self.last)
+            return mine + fin[turn, 0].astype(F32) + fin[turn, 1].astype(F32)
+
+    first_rows = Rows(0)
+
     def forward_pair(p):
         s0, s1 = slot(*PAIRS[p][0]), slot(*PAIRS[p][1])
         for ref, dense in ((slot_in, dense_in), (slot_out, dense_out)):
@@ -203,6 +259,14 @@
         act, der = gelu_and_slope(pre)
         slope[p] = der.astype(BF16).reshape(4, 2 * R, 2 * U)
         act = act.astype(BF16)
+        if p == 7:
+            for dz in (2, 1, 3, 0):
+                at = PLACE[dz]
+                some = act[at * 2 * R:(at + 1) * 2 * R]
+                for n in range(0, D, 256):
+                    acc[at, :, n:n + 256] += mm(some, dense_out[p, :, n:n + 256])
+                first_rows.offer(dz)
+            return
         for n in range(0, D, 256):
             part = mm(act, dense_out[p, :, n:n + 256]).reshape(4, 2 * R, 256)
             if p == 0:
@@ -264,63 +328,7 @@
     got_halves("out", (2, 2))
     forward_pair(7)
 
-    lo, hi = slice(0, H), slice(H, D)
-    own, other = slice(0, R), slice(R, 2 * R)
-
-    class Rows:
-        def __init__(self, turn):
-            self.turn = turn
-            self.core = {}
-            self.last = []
-
-        def offer(self, dz):
-            stage[dz] = acc[PLACE[dz], other, :].astype(BF16)
-            self.core[dz] = send(stage.at[dz], core_in.at[self.turn, dz], core)
-
-        def both(self, dz, columns):
-            theirs = core_in[self.turn, dz, :, columns].astype(F32)
-            return acc[PLACE[dz], own, columns] + theirs
-
-        def far(self):
-            turn = self.turn
-            self.core[2].wait_recv()
-            direct[0] = self.both(2, slice(0, D)).astype(BF16)
-            self.up = send(direct.at[0, :, lo], hop.at[turn, 0], z_fwd)
-            self.down = send(direct.at[0, :, hi], hop.at[turn, 1], z_bwd)
-
-        def near_up(self):
-            turn = self.turn
-            self.core[1].wait_recv()
-            direct[1, :, hi] = self.both(1, hi).astype(BF16)
-            self.last.append(send(direct.at[1, :, hi], fin.at[turn, 0, :, hi], z_fwd))
-
-        def near_down(self):
-            turn = self.turn
-            self.core[3].wait_recv()
-            direct[2, :, lo] = self.both(3, lo).astype(BF16)
-            self.last.append(send(direct.at[2, :, lo], fin.at[turn, 1, :, lo], z_bwd))
-
-        def hops(self):
-            turn = self.turn
-            self.up.wait_recv()
-            total = self.both(1, lo) + hop[turn, 0].astype(F32)
-            direct[1, :, lo] = total.astype(BF16)
-            self.last.append(send(direct.at[1, :, lo], fin.at[turn, 0, :, lo], z_fwd))
-            self.down.wait_recv()
-            total = self.both(3, hi) + hop[turn, 1].astype(F32)
-            direct[2, :, hi] = total.astype(BF16)
-            self.last.append(send(direct.at[2, :, hi], fin.at[turn, 1, :, hi], z_bwd))
-
-        def result(self):
-            turn = self.turn
-            self.core[0].wait_recv()
-            mine = self.both(0, slice(0, D))
-            arrived(self.last)
-            return mine + fin[turn, 0].astype(F32) + fin[turn, 1].astype(F32)
-
-    rows = Rows(0)
-    for dz in (2, 1, 3, 0):
-        rows.offer(dz)
+    rows = first_rows
     rows.far()
     rows.near_up()
     rows.near_down()
@@ -347,15 +355,16 @@
     arrived(text_core)
     scaling = scale[0]
     offset = bias[0]
-    same = lax.broadcasted_iota(jnp.int32, (R, R), 0) == lax.broadcasted_iota(jnp.int32, (R, R), 1)
+    pairs = (R, 8 * R)
+    same = lax.broadcasted_iota(jnp.int32, pairs, 0) == lax.broadcasted_iota(jnp.int32, pairs, 1)
 
     def other_side(mine, theirs, slabs, positive):
         total = None
-        for n in range(4 * slabs):
-            block = theirs[n // 4, n % 4]
+        for q in range(0, slabs, 2):
+            block = theirs[q:q + 2].reshape(8 * R, E)
             logits = scaling * mm_nt(mine, block) + offset
             soft = jax.nn.sigmoid(logits)
-            if positive and n == 0:
+            if positive and q == 0:
                 soft = jnp.where(same, -jax.nn.sigmoid(-logits), soft)
             term = mm(soft.astype(BF16), block)
             total = term if total is None else total + term
@@ -411,6 +420,8 @@
     expand(1, 3)
     arrived(pd_far)
     pd_core[2] = send(pd.at[0, PLACE[2]], pd.at[1, PLACE[2]], core)
+    arrived(rs_in)
+    rs_core = send(rs.at[0], rs.at[1], core)
     hidden_back(1, 3)
     pd_core[2].wait_recv()
     expand(3, 4)
@@ -420,10 +431,13 @@
     rows = Rows(1)
     input_back(2)
     rows.offer(2)
-    arrived(rs_in)
-    rs_core = send(rs.at[0], rs.at[1], core)
-    arrived(embeds_first)
-    embeds_core = send(eall.at[0], eall.at[1], core)
+    rs_core.wait_recv()
+    columns = pl.ds(pl.multiple_of(mp * 256, 128), 256)
+    term = mm_tn(rs[...].reshape(8 * R, H), pd[:, :, :, columns].reshape(8 * R, 256))
+    for n in range(16):
+        pg[n % 4, n // 4] = term[n * 56:(n + 1) * 56, :].astype(BF16)
+    pg_first = [send(pg.at[(xi + k) % 4], pg_in.at[k - 1], along_x[k]) for k in (1, 2, 3)]
+
     input_back(1)
     rows.offer(1)
     rows.far()
@@ -431,19 +445,14 @@
     rows.offer(3)
     rows.near_up()
     rows.near_down()
-
-    rs_core.wait_recv()
-    columns = pl.ds(pl.multiple_of(mp * 256, 128), 256)
-    term = mm_tn(rs[...].reshape(8 * R, H), pd[:, :, :, columns].reshape(8 * R, 256))
-    for n in range(16):
-        pg[n % 4, n // 4] = term[n * 56:(n + 1) * 56, :].astype(BF16)
-    pg_first = [send(pg.at[(xi + k) % 4], pg_in.at[k - 1], along_x[k]) for k in (1, 2, 3)]
     rows.hops()
+    arrived(embeds_first)
+    embeds_core = send(eall.at[0], eall.at[1], core)
+    input_back(0)
+    rows.offer(0)
     embeds_core.wait_recv()
     unit_part[0] = other_side(tall[1, 0], eall, 2, False).astype(BF16)
     unit_far = send(unit_part.at[0], unit_part.at[1], z_far)
-    input_back(0)
-    rows.offer(0)
 
     arrived(pg_first)
     part = pg[xi].astype(F32)
@@ -454,8 +463,8 @@
 
     tf, text_inv = text_parts()
     unit_grad = other_side(tall[0, 0], eall, 2, True)
+    _, normed, inv_std = norm_rows(own_row)
     input_grad = rows.result()
-    _, normed, inv_std = norm_rows(own_row)
     scaled = input_grad * gain[...].reshape(1, D)
     shift = scaled - jnp.mean(scaled, axis=-1, keepdims=True)
     shift = shift - normed * jnp.mean(scaled * normed, axis=-1, keepdims=True)

time: 155 us -> 155 us (level)
  no operation moved by 1% of the time
where the time goes in v4:
time: 155 us
  Pallas kernels  153 us (99%)
  between operations  1.93 us (1%)
    pallas_call x1, Pallas kernels, per_device(): pl.pallas_call(kernel, out_shape=(jax.ShapeDtypeStruct((R, D), F32), jax....  151 us

profile of v4, /device:TPU:1, one launch (start us, length us, event | category | flops | bytes accessed | tf_op | source)
XLA Modules:
  0.0 155.0 jit_solution(7222387850575171194)
XLA Ops:
  1.9 150.9 %shard_map.103 = (f32[80,1792]{1,0:T(8,128)}, f32[56,256]{1,0:T(8,128)}, f32[80,1024]{1,0:T(8,128)}) custom-call(bf16[320,1792]{1,0:T(8,128)(2,1)} %pooled.1, f32[1792]{0:T(1024)} %gain.1, bf16[120,1792]{1,0:T(8,128)(2,1)} %w_in.1, bf16[120,1792]{1,0:T(8,128)(2,1)} %w_out.1, bf16[1792,1024]{1,0:T(8,128)(2,1)} %proj_hbm.1, bf16[80,1024]{1,0:T(8,128)(2,1)} %text.1, ...), custom_call_target="tpu_custom_call" | custom-call | tf_op jit(solution)/shard_map/pallas_call | solution.py:499
  152.9 2.1 %shard_map.104 = (f32[80,1792]{1,0:T(8,128)}, f32[56,256]{1,0:T(8,128)}, f32[80,1024]{1,0:T(8,128)}) custom-call(f32[80,1792]{1,0:T(8,128)} %get-tuple-element.6.d_in, f32[56,256]{1,0:T(8,128)} %get-tuple-element.7.p_in, f32[80,1024]{1,0:T(8,128)} %get-tuple-element.8.t_in), custom_call_target="tpu_custom_call" | custom-call | tf_op jit(solution)/shard_map/pallas_call | solution.py:541

commit v5 on v3

--- a/solution.py
+++ b/solution.py
@@ -347,15 +347,16 @@
     arrived(text_core)
     scaling = scale[0]
     offset = bias[0]
-    same = lax.broadcasted_iota(jnp.int32, (R, R), 0) == lax.broadcasted_iota(jnp.int32, (R, R), 1)
+    pairs = (R, 8 * R)
+    same = lax.broadcasted_iota(jnp.int32, pairs, 0) == lax.broadcasted_iota(jnp.int32, pairs, 1)
 
     def other_side(mine, theirs, slabs, positive):
         total = None
-        for n in range(4 * slabs):
-            block = theirs[n // 4, n % 4]
+        for q in range(0, slabs, 2):
+            block = theirs[q:q + 2].reshape(8 * R, E)
             logits = scaling * mm_nt(mine, block) + offset
             soft = jax.nn.sigmoid(logits)
-            if positive and n == 0:
+            if positive and q == 0:
                 soft = jnp.where(same, -jax.nn.sigmoid(-logits), soft)
             term = mm(soft.astype(BF16), block)
             total = term if total is None else total + term
@@ -454,8 +455,8 @@
 
     tf, text_inv = text_parts()
     unit_grad = other_side(tall[0, 0], eall, 2, True)
+    _, normed, inv_std = norm_rows(own_row)
     input_grad = rows.result()
-    _, normed, inv_std = norm_rows(own_row)
     scaled = input_grad * gain[...].reshape(1, D)
     shift = scaled - jnp.mean(scaled, axis=-1, keepdims=True)
     shift = shift - normed * jnp.mean(scaled * normed, axis=-1, keepdims=True)

time: 155 us -> 155 us (level)
  no operation moved by 1% of the time
where the time goes in v5:
time: 155 us
  Pallas kernels  153 us (99%)
  between operations  1.93 us (1%)
    pallas_call x1, Pallas kernels, per_device(): pl.pallas_call(kernel, out_shape=(jax.ShapeDtypeStruct((R, D), F32), jax....  151 us

profile of v5, /device:TPU:1, one launch (start us, length us, event | category | flops | bytes accessed | tf_op | source)
XLA Modules:
  0.0 154.8 jit_solution(5005210352706920223)
XLA Ops:
  1.9 150.7 %shard_map.103 = (f32[80,1792]{1,0:T(8,128)}, f32[56,256]{1,0:T(8,128)}, f32[80,1024]{1,0:T(8,128)}) custom-call(bf16[320,1792]{1,0:T(8,128)(2,1)} %pooled.1, f32[1792]{0:T(1024)} %gain.1, bf16[120,1792]{1,0:T(8,128)(2,1)} %w_in.1, bf16[120,1792]{1,0:T(8,128)(2,1)} %w_out.1, bf16[1792,1024]{1,0:T(8,128)(2,1)} %proj_hbm.1, bf16[80,1024]{1,0:T(8,128)(2,1)} %text.1, ...), custom_call_target="tpu_custom_call" | custom-call | tf_op jit(solution)/shard_map/pallas_call | solution.py:491
  152.7 2.1 %shard_map.104 = (f32[80,1792]{1,0:T(8,128)}, f32[56,256]{1,0:T(8,128)}, f32[80,1024]{1,0:T(8,128)}) custom-call(f32[80,1792]{1,0:T(8,128)} %get-tuple-element.6.d_in, f32[56,256]{1,0:T(8,128)} %get-tuple-element.7.p_in, f32[80,1024]{1,0:T(8,128)} %get-tuple-element.8.t_in), custom_call_target="tpu_custom_call" | custom-call | tf_op jit(solution)/shard_map/pallas_call | solution.py:533

commit v6 on v5

--- a/solution.py
+++ b/solution.py
@@ -423,8 +423,6 @@
     rows.offer(2)
     arrived(rs_in)
     rs_core = send(rs.at[0], rs.at[1], core)
-    arrived(embeds_first)
-    embeds_core = send(eall.at[0], eall.at[1], core)
     input_back(1)
     rows.offer(1)
     rows.far()
@@ -440,11 +438,13 @@
         pg[n % 4, n // 4] = term[n * 56:(n + 1) * 56, :].astype(BF16)
     pg_first = [send(pg.at[(xi + k) % 4], pg_in.at[k - 1], along_x[k]) for k in (1, 2, 3)]
     rows.hops()
+    arrived(embeds_first)
+    embeds_core = send(eall.at[0], eall.at[1], core)
+    input_back(0)
+    rows.offer(0)
     embeds_core.wait_recv()
     unit_part[0] = other_side(tall[1, 0], eall, 2, False).astype(BF16)
     unit_far = send(unit_part.at[0], unit_part.at[1], z_far)
-    input_back(0)
-    rows.offer(0)
 
     arrived(pg_first)
     part = pg[xi].astype(F32)

time: 155 us -> 155 us (level)
  no operation moved by 1% of the time
where the time goes in v6:
time: 155 us
  Pallas kernels  153 us (99%)
  between operations  1.93 us (1%)
    pallas_call x1, Pallas kernels, per_device(): pl.pallas_call(kernel, out_shape=(jax.ShapeDtypeStruct((R, D), F32), jax....  151 us

profile of v6, /device:TPU:1, one launch (start us, length us, event | category | flops | bytes accessed | tf_op | source)
XLA Modules:
  0.0 154.8 jit_solution(13670081799492713876)
XLA Ops:
  1.9 150.7 %shard_map.103 = (f32[80,1792]{1,0:T(8,128)}, f32[56,256]{1,0:T(8,128)}, f32[80,1024]{1,0:T(8,128)}) custom-call(bf16[320,1792]{1,0:T(8,128)(2,1)} %pooled.1, f32[1792]{0:T(1024)} %gain.1, bf16[120,1792]{1,0:T(8,128)(2,1)} %w_in.1, bf16[120,1792]{1,0:T(8,128)(2,1)} %w_out.1, bf16[1792,1024]{1,0:T(8,128)(2,1)} %proj_hbm.1, bf16[80,1024]{1,0:T(8,128)(2,1)} %text.1, ...), custom_call_target="tpu_custom_call" | custom-call | tf_op jit(solution)/shard_map/pallas_call | solution.py:491
  152.7 2.1 %shard_map.104 = (f32[80,1792]{1,0:T(8,128)}, f32[56,256]{1,0:T(8,128)}, f32[80,1024]{1,0:T(8,128)}) custom-call(f32[80,1792]{1,0:T(8,128)} %get-tuple-element.6.d_in, f32[56,256]{1,0:T(8,128)} %get-tuple-element.7.p_in, f32[80,1024]{1,0:T(8,128)} %get-tuple-element.8.t_in), custom_call_target="tpu_custom_call" | custom-call | tf_op jit(solution)/shard_map/pallas_call | solution.py:533
